TPU v7x, 128 devices: a whole 4x4x4 slice. The times are simulated.
128 devices in a mesh: space: 64 (over z, y, x), view: 2 (over core).
Axes of the slice: x: 4, y: 4, z: 4, core: 2. Of those that a mesh axis runs over, the one named last changes fastest.
Arguments:
- params: float32 [59, 131072], P(None, 'space')
- camera: float32 [2, 3, 4], P('view'), as said below
- eye_point: float32 [2, 3], P('view'), may hold values from -9 to 9
- tile_of: int32 [2, 512], P('view', 'space'), may hold values from 0 to 511, as said below
- fetch: int32 [2, 64, 64, 16], P('view', 'space'), may hold values from 0 to 2047, as said below
- lists: int32 [2, 512, 256], P('view', 'space'), may hold values from 0 to 1023
- counts: int32 [2, 512], P('view', 'space'), may hold values from 1 to 256
- target: float32 [2, 512, 3, 256], P('view', 'space'), may hold values from -2 to 2
Outputs:
- rendered: float32 [2, 512, 3, 256], P('view', 'space')
- grads: float32 [59, 131072], P(None, 'space')
Inputs may be any that keep to these rules, and one draw needn't show every extreme that they name: `fetch`: over both views and all renderers, the entries for one owner name each of its 2048 Gaussians exactly once. `tile_of`: each view's row names every tile once; the slots of one renderer cover a rectangle of adjacent tiles. `camera`: in rows 0 and 1, columns 0 and 1 hold diagonal entries of 0.6 to 1.1 and off-diagonal entries of magnitude at most 0.4.
All inputs are finite; a program needn't handle non-finite values.
Results may differ from a plain program's by a relative error of at most 0.0003.
Values sent between devices are 32-bit elements; how exact they have to be, the bound alone decides.
A program may use at most 192 MiB of HBM per device.

v0:
```python
import jax
import jax.numpy as jnp
from jax import lax
from jax.sharding import PartitionSpec as P

DILATE = 0.3 / 262144.0
HARM_ZERO = 0.28209479177387814
HARM_ONE = 0.4886025119029199
HARM_TWO = (
    1.0925484305920792,
    -1.0925484305920792,
    0.31539156525252005,
    -1.0925484305920792,
    0.5462742152960396,
)
HARM_THREE = (
    -0.5900435899266435,
    2.890611442640554,
    -0.4570457994644658,
    0.3731763325901154,
    -0.4570457994644658,
    1.445305721320277,
    -0.5900435899266435,
)


def harmonics(dir_x, dir_y, dir_z):
    sq_x, sq_y, sq_z = (dir_x * dir_x, dir_y * dir_y, dir_z * dir_z)
    return [
        HARM_ZERO * jnp.ones_like(dir_x),
        -HARM_ONE * dir_y,
        HARM_ONE * dir_z,
        -HARM_ONE * dir_x,
        HARM_TWO[0] * dir_x * dir_y,
        HARM_TWO[1] * dir_y * dir_z,
        HARM_TWO[2] * (2.0 * sq_z - sq_x - sq_y),
        HARM_TWO[3] * dir_x * dir_z,
        HARM_TWO[4] * (sq_x - sq_y),
        HARM_THREE[0] * dir_y * (3.0 * sq_x - sq_y),
        HARM_THREE[1] * dir_x * dir_y * dir_z,
        HARM_THREE[2] * dir_y * (4.0 * sq_z - sq_x - sq_y),
        HARM_THREE[3] * dir_z * (2.0 * sq_z - 3.0 * sq_x - 3.0 * sq_y),
        HARM_THREE[4] * dir_x * (4.0 * sq_z - sq_x - sq_y),
        HARM_THREE[5] * dir_z * (sq_x - sq_y),
        HARM_THREE[6] * dir_x * (sq_x - 3.0 * sq_y),
    ]


def project(params, camera, eye_point):
    centre = params[0:3]
    scales = jnp.exp(params[3:6])
    quat = params[6:10]
    quat = quat / jnp.sqrt(jnp.sum(quat * quat, axis=0, keepdims=True))
    q_w, q_x, q_y, q_z = (quat[0], quat[1], quat[2], quat[3])
    rotation = [
        [
            1.0 - 2.0 * (q_y * q_y + q_z * q_z),
            2.0 * (q_x * q_y - q_w * q_z),
            2.0 * (q_x * q_z + q_w * q_y),
        ],
        [
            2.0 * (q_x * q_y + q_w * q_z),
            1.0 - 2.0 * (q_x * q_x + q_z * q_z),
            2.0 * (q_y * q_z - q_w * q_x),
        ],
        [
            2.0 * (q_x * q_z - q_w * q_y),
            2.0 * (q_y * q_z + q_w * q_x),
            1.0 - 2.0 * (q_x * q_x + q_y * q_y),
        ],
    ]
    jacob = [
        [
            (
                camera[row, 0] * rotation[0][col]
                + camera[row, 1] * rotation[1][col]
                + camera[row, 2] * rotation[2][col]
            )
            * scales[col]
            for col in range(3)
        ]
        for row in range(2)
    ]
    cov_xx = (
        jacob[0][0] * jacob[0][0] + jacob[0][1] * jacob[0][1] + jacob[0][2] * jacob[0][2] + DILATE
    )
    cov_xy = jacob[0][0] * jacob[1][0] + jacob[0][1] * jacob[1][1] + jacob[0][2] * jacob[1][2]
    cov_yy = (
        jacob[1][0] * jacob[1][0] + jacob[1][1] * jacob[1][1] + jacob[1][2] * jacob[1][2] + DILATE
    )
    determinant = cov_xx * cov_yy - cov_xy * cov_xy
    screen_x = (
        camera[0, 0] * centre[0]
        + camera[0, 1] * centre[1]
        + camera[0, 2] * centre[2]
        + camera[0, 3]
    )
    screen_y = (
        camera[1, 0] * centre[0]
        + camera[1, 1] * centre[1]
        + camera[1, 2] * centre[2]
        + camera[1, 3]
    )
    opacity = jax.nn.sigmoid(params[10])
    offset = centre - eye_point[:, None]
    inverse = 1.0 / jnp.sqrt(jnp.sum(offset * offset, axis=0) + 1.0)
    basis = jnp.stack(harmonics(offset[0] * inverse, offset[1] * inverse, offset[2] * inverse))
    coeffs = params[11:59].reshape(16, 3, params.shape[1])
    colour = jnp.maximum(jnp.sum(basis[:, None, :] * coeffs, axis=0) + 0.5, 0.0)
    return jnp.stack(
        [
            screen_x,
            screen_y,
            cov_yy / determinant,
            -cov_xy / determinant,
            cov_xx / determinant,
            opacity,
            colour[0],
            colour[1],
            colour[2],
        ]
    )


def composite(entries, count, tile, cumulate):
    pixel = jnp.arange(256, dtype=jnp.int32)
    col_pix = tile % 32 * 16 + pixel % 16
    row_pix = tile // 32 * 16 + pixel // 16
    pos_x = (col_pix.astype(jnp.float32) + 0.5) / 512.0
    pos_y = (row_pix.astype(jnp.float32) + 0.5) / 512.0
    off_x = pos_x[:, None] - entries[0][None, :]
    off_y = pos_y[:, None] - entries[1][None, :]
    power = (
        -0.5 * (entries[2][None, :] * off_x * off_x + entries[4][None, :] * off_y * off_y)
        - entries[3][None, :] * off_x * off_y
    )
    alphas = entries[5][None, :] * jnp.exp(power)
    live = jnp.arange(entries.shape[1], dtype=jnp.int32) < count
    alphas = jnp.where(live[None, :], alphas, 0.0)
    before = cumulate(jnp.log1p(-alphas))
    weights = jnp.exp(before) * alphas
    return jnp.sum(weights[None, :, :] * entries[6:9][:, None, :], axis=2)


def render_tiles(sectioning, lists, counts, tiles):
    length = lists.shape[1]
    order = jnp.arange(length, dtype=jnp.int32)
    upper = (order[:, None] < order[None, :]).astype(jnp.float32)

    def cumulate(logs):
        return jnp.dot(logs, upper, precision=lax.Precision.HIGHEST)

    entries = sectioning[:, lists]

    def one_tile(tile_entries, count, tile):
        return composite(tile_entries, count, tile, cumulate)

    return jax.vmap(one_tile, in_axes=(1, 0, 0))(entries, counts, tiles)


def on_device(params, camera, eye_point, tile_of, fetch, lists, counts, target):
    owners = lax.axis_size("space")
    shard_len = params.shape[1]
    request = fetch[0, 0]
    projected, back_project = jax.vjp(
        lambda values: project(values, camera[0], eye_point[0]), params
    )
    everything = lax.all_gather(projected, "space", axis=1, tiled=True)
    flat_ids = (jnp.arange(owners, dtype=jnp.int32)[:, None] * shard_len + request).reshape(-1)
    sectioning = everything[:, flat_ids]
    rendered, back_render = jax.vjp(
        lambda rows: render_tiles(rows, lists[0], counts[0], tile_of[0]), sectioning
    )
    (row_cotangent,) = back_render((rendered - target[0]) / 256.0)
    dense = jnp.zeros((9, owners * shard_len), jnp.float32).at[:, flat_ids].add(row_cotangent)
    proj_grad = lax.psum_scatter(dense, "space", scatter_dimension=1, tiled=True)
    (param_grad,) = back_project(proj_grad)
    summed = lax.psum(param_grad, "view")
    return (rendered[None], summed)


def solution(mesh):
    placed = (
        P(None, "space"),
        P("view", None, None),
        P("view", None),
        P("view", "space"),
        P("view", "space", None, None),
        P("view", "space", None),
        P("view", "space"),
        P("view", "space", None, None),
    )
    return jax.shard_map(
        on_device,
        mesh=mesh,
        in_specs=placed,
        out_specs=(P("view", "space", None, None), P(None, "space")),
        check_vma=False,
    )
```

profile of v0, /device:TPU:1, one launch (start us, length us, event | category | flops | bytes accessed | tf_op | source)
XLA Modules:
  0.0 680.7 jit_solution(2149426540691532369)
XLA Ops:
  7.2 0.9 multiply_reduce_fusion.8
  8.2 1.1 slice.158
  10.6 1.0 multiply_reduce_fusion.7
  11.7 0.9 slice_divide_fusion
  17.1 3.9 fusion.92
  21.1 6.1 add_divide_fusion
  27.2 2.3 stack.9
  30.0 3.8 sort
  34.0 78.1 %all-gather.2.cloned.1.call-done = f32[9,131072]{1,0:T(8,128)} async-done(((f32[9,2048]{1,0:T(8,128)}), f32[9,131072]{1,0:T(8,128)}) %all-gather.2.cloned.1.call-update) | async-done | bytes 4718608 | tf_op jit(solution)/shard_map/all_gather | solution.py:168
  112.1 31.5 %copy.281 = f32[9,131072]{0,1:T(8,128)} copy(f32[9,131072]{1,0:T(8,128)} %all-gather.2.cloned.1.call-done) | data formatting | bytes 9437184 | tf_op jit(solution)/shard_map/all_gather | solution.py:168
  143.6 10.5 %gather_fusion = f32[1024,9]{1,0:T(8,128)S(1)} fusion(f32[9,131072]{0,1:T(8,128)} %copy.281, s32[1024]{0:T(1024)S(1)} %broadcast_clamp_fusion.2), kind=kCustom, calls=%fused_computation | custom fusion | bytes 77824 | tf_op jit(solution)/shard_map/gather | solution.py:170
  154.1 5.5 gather_fusion.1
  160.0 3.8 exponential_multiply_fusion
  163.8 0.9 multiply_reduce_fusion.2
  164.7 1.3 multiply_reduce_fusion.1
  166.1 6.3 fusion.16
  173.0 11.8 %scatter_custom_fusion = f32[9,1024]{0,1:T(8,128)S(1)} fusion(s32[2048]{0:T(1024)S(1)} %bitcast.118, f32[2048,9]{1,0:T(8,128)S(1)} %bitcast.103, f32[]{:T(128)} %constant.41.clone.1), kind=kCustom, calls=%fused_computation.61 | custom fusion | flops 18432 | bytes 36868 | tf_op jit(solution)/shard_map/transpose(jvp())/scatter-add | solution.py:153
  184.8 42.3 %scatter_custom_fusion.1 = f32[9,131072]{0,1:T(8,128)} fusion(s32[1024]{0:T(1024)S(1)} %get-tuple-element.14, f32[]{:T(128)} %constant.41.clone.1, f32[1024,9]{1,0:T(8,128)S(1)} %bitcast.105, s32[1024]{0:T(1024)S(1)} %broadcast_clamp_fusion.1), kind=kCustom, calls=%fused_computation.5 | custom fusion | flops 9216 | bytes 4718596 | tf_op jit(solution)/shard_map/scatter-add | solution.py:175
  227.1 36.9 %copy.293 = f32[9,131072]{1,0:T(8,128)} copy(f32[9,131072]{0,1:T(8,128)} %scatter_custom_fusion.1) | data formatting | bytes 9437184 | tf_op jit(solution)/shard_map/scatter-add | solution.py:175
  264.1 321.7 %reduce-scatter.2.cloned.1.call-done = f32[9,2048]{1,0:T(8,128)} async-done(((f32[9,131072]{1,0:T(8,128)}), f32[9,2048]{1,0:T(8,128)}) %reduce-scatter.2.cloned.1.call-update) | async-done | bytes 73744 | tf_op jit(solution)/shard_map/reduce_scatter | solution.py:176
  585.9 4.8 fusion.51
  591.7 1.0 multiply_add_fusion.8
  592.7 1.0 multiply_add_fusion.7
  593.7 3.9 add_add_fusion.10
  597.8 2.5 add_add_fusion.9
  600.3 2.6 multiply_add_fusion.6
  602.9 1.0 multiply_reduce_fusion.6
  603.9 1.0 add_add_fusion.1
  605.1 0.9 add_multiply_fusion
  606.1 0.9 pad_add_fusion
  607.6 64.6 %all-reduce.36.cloned.1.call-done = f32[59,2048]{1,0:T(8,128)} async-done(((f32[59,2048]{1,0:T(8,128)}), f32[59,2048]{1,0:T(8,128)}) %all-reduce.36.cloned.1.call-update) | async-done | bytes 483344 | tf_op jit(solution)/shard_map/psum | solution.py:178
  672.3 1.9 copy.303
  (79 shorter events, 5.9 us)
Async XLA Ops:
  7.2 22.6 %copy-start.1 = (s32[1,1,64,16]{2,3,1,0:T(8,128)S(1)}, s32[1,1,64,16]{2,3,1,0:T(8,128)}, u32[]{:S(2)}) copy-start(s32[1,1,64,16]{2,3,1,0:T(8,128)} %param.12) | copy-start | bytes 12292
  7.2 104.9 %all-gather.2.cloned.1.call-start = ((), (), s32[]{:S(2)}) async-start(), calls=%async_computation.1 | async-start | bytes 8519680 | tf_op jit(solution)/shard_map/all_gather | solution.py:168
  8.2 21.7 %copy-start.2 = (s32[1,8,256]{2,1,0:T(8,128)S(1)}, s32[1,8,256]{2,1,0:T(8,128)}, u32[]{:S(2)}) copy-start(s32[1,8,256]{2,1,0:T(8,128)} %param.13) | copy-start | bytes 24580
  8.2 25.6 %copy-start.4 = (s32[1,8]{1,0:T(1,128)S(1)}, s32[1,8]{1,0:T(1,128)}, u32[]{:S(2)}) copy-start(s32[1,8]{1,0:T(1,128)} %param.11) | copy-start | bytes 100
  8.2 25.6 %copy-start.3 = (s32[1,8]{1,0:T(1,128)S(1)}, s32[1,8]{1,0:T(1,128)}, u32[]{:S(2)}) copy-start(s32[1,8]{1,0:T(1,128)} %param.14) | copy-start | bytes 100
  29.5 556.4 %reduce-scatter.2.cloned.1.call-start = ((), (), s32[]{:S(2)}) async-start(), calls=%async_computation.2 | async-start | bytes 8519680 | tf_op jit(solution)/shard_map/reduce_scatter | solution.py:176
  163.8 0.9 copy-start
  264.1 408.2 %all-reduce.36.cloned.1.call-start = ((), (), s32[]{:S(2)}) async-start(), calls=%async_computation.3 | async-start | bytes 1048576 | tf_op jit(solution)/shard_map/psum | solution.py:178
Sparse Core Ops, SparseCore 0:
  29.6 82.4 all-gather.1
  264.2 321.6 reduce-scatter.1
  607.1 65.0 all-reduce.35
where the time goes:
time: 683 us; the launch traced here: 681 us
  waiting for transfers between devices  465 us (68%)
  other arithmetic  94.5 us (14%)
  local copies, waits for them, and re-layouts  93.4 us (14%)
  between operations  18 us (3%)
  matrix products  10.1 us (1%)
    reduce_scatter x1, waiting for transfers between devices, on_device(): lax.psum_scatter(dense, 'space', scatter_dimension=1, tiled=True)  322 us
    all_gather x1, waiting for transfers between devices, on_device(): everything = lax.all_gather(projected, 'space', axis=1, tiled=True)  78.1 us
    psum x1, waiting for transfers between devices, on_device(): summed = lax.psum(param_grad, 'view')  64.6 us
    scatter-add x3, other arithmetic, on_device(): jnp.zeros((9, owners * shard_len), jnp.float32).at[:, flat_ids]  46.1 us
    scatter-add x2, local copies, waits for them, and re-layouts, on_device(): jnp.zeros((9, owners * shard_len), jnp.float32).at[:, flat_ids]  36.9 us
    all_gather x1, local copies, waits for them, and re-layouts, on_device(): everything = lax.all_gather(projected, 'space', axis=1, tiled=True)  31.5 us
  transfers between devices with their start and end apart: 3, of which 3 were waited for; matrix products, arithmetic and copies ran while one was open for 1% of the time, Pallas kernels for 0%

commit v1 on v0

v1 whole, which is shorter than its diff:
```python
import functools

import jax
import jax.numpy as jnp
from jax import lax
from jax.experimental import pallas as pl
from jax.experimental.pallas import tpu as pltpu
from jax.sharding import PartitionSpec as P

DILATE = 0.3 / 262144.0
HARM_ZERO = 0.28209479177387814
HARM_ONE = 0.4886025119029199
HARM_TWO = (
    1.0925484305920792,
    -1.0925484305920792,
    0.31539156525252005,
    -1.0925484305920792,
    0.5462742152960396,
)
HARM_THREE = (
    -0.5900435899266435,
    2.890611442640554,
    -0.4570457994644658,
    0.3731763325901154,
    -0.4570457994644658,
    1.445305721320277,
    -0.5900435899266435,
)
LOG2E = 1.4426950408889634
MESH = pl.DeviceIdType.MESH
F32 = jnp.float32
BF16 = jnp.bfloat16

N = 64
CAP = 16
TILES = 8
K = 256
PX = 256
ROWS = 59
PITCH = 64
COLS = 16
FEATS = 9
GROUP = 32
MOMS = 16
CHUNK = 32


def harmonics(dir_x, dir_y, dir_z):
    sq_x, sq_y, sq_z = (dir_x * dir_x, dir_y * dir_y, dir_z * dir_z)
    return [
        HARM_ZERO * jnp.ones_like(dir_x),
        -HARM_ONE * dir_y,
        HARM_ONE * dir_z,
        -HARM_ONE * dir_x,
        HARM_TWO[0] * dir_x * dir_y,
        HARM_TWO[1] * dir_y * dir_z,
        HARM_TWO[2] * (2.0 * sq_z - sq_x - sq_y),
        HARM_TWO[3] * dir_x * dir_z,
        HARM_TWO[4] * (sq_x - sq_y),
        HARM_THREE[0] * dir_y * (3.0 * sq_x - sq_y),
        HARM_THREE[1] * dir_x * dir_y * dir_z,
        HARM_THREE[2] * dir_y * (4.0 * sq_z - sq_x - sq_y),
        HARM_THREE[3] * dir_z * (2.0 * sq_z - 3.0 * sq_x - 3.0 * sq_y),
        HARM_THREE[4] * dir_x * (4.0 * sq_z - sq_x - sq_y),
        HARM_THREE[5] * dir_z * (sq_x - sq_y),
        HARM_THREE[6] * dir_x * (sq_x - 3.0 * sq_y),
    ]


def project(rows, camera, eye):
    centre = rows[0:3]
    scales = [jnp.exp(row) for row in rows[3:6]]
    quat = rows[6:10]
    norm = lax.rsqrt(sum(q * q for q in quat))
    q_w, q_x, q_y, q_z = [q * norm for q in quat]
    rotation = [
        [
            1.0 - 2.0 * (q_y * q_y + q_z * q_z),
            2.0 * (q_x * q_y - q_w * q_z),
            2.0 * (q_x * q_z + q_w * q_y),
        ],
        [
            2.0 * (q_x * q_y + q_w * q_z),
            1.0 - 2.0 * (q_x * q_x + q_z * q_z),
            2.0 * (q_y * q_z - q_w * q_x),
        ],
        [
            2.0 * (q_x * q_z - q_w * q_y),
            2.0 * (q_y * q_z + q_w * q_x),
            1.0 - 2.0 * (q_x * q_x + q_y * q_y),
        ],
    ]
    jacob = [
        [
            (
                camera[row][0] * rotation[0][col]
                + camera[row][1] * rotation[1][col]
                + camera[row][2] * rotation[2][col]
            )
            * scales[col]
            for col in range(3)
        ]
        for row in range(2)
    ]
    cov_xx = sum(j * j for j in jacob[0]) + DILATE
    cov_xy = sum(j * i for j, i in zip(jacob[0], jacob[1]))
    cov_yy = sum(j * j for j in jacob[1]) + DILATE
    inv_det = 1.0 / (cov_xx * cov_yy - cov_xy * cov_xy)
    screen = [
        camera[row][0] * centre[0]
        + camera[row][1] * centre[1]
        + camera[row][2] * centre[2]
        + camera[row][3]
        for row in range(2)
    ]
    logit = rows[10]
    log_opacity = jnp.minimum(logit, 0.0) - jnp.log1p(jnp.exp(-jnp.abs(logit)))
    offset = [c - e for c, e in zip(centre, eye)]
    inverse = lax.rsqrt(sum(o * o for o in offset) + 1.0)
    basis = harmonics(*[o * inverse for o in offset])
    colours = [
        jnp.maximum(sum(b * rows[11 + 3 * l + c] for l, b in enumerate(basis)) + 0.5, 0.0)
        for c in range(3)
    ]
    return [
        *screen,
        cov_yy * inv_det,
        -cov_xy * inv_det,
        cov_xx * inv_det,
        log_opacity,
        *colours,
    ]


def split(value, parts):
    pieces = []
    for _ in range(parts - 1):
        piece = value.astype(BF16).astype(F32)
        pieces.append(piece)
        value = value - piece
    return [*pieces, value.astype(BF16).astype(F32)]


def split_low(value, parts):
    pieces = []
    for _ in range(parts - 1):
        piece = value.astype(BF16)
        pieces.append(piece)
        value = value - piece.astype(F32)
    return [*pieces, value.astype(BF16)]


def iota(shape, dim):
    return lax.broadcasted_iota(jnp.int32, shape, dim)


def pick(table, row, lane):
    shape = row.shape
    found = jnp.zeros(shape, F32)
    for r in range(16):
        line = jnp.broadcast_to(table[r : r + 1, :], shape)
        found = jnp.where(row == r, jnp.take_along_axis(line, lane, axis=1), found)
    return found


def dot_nt(left, right):
    return lax.dot_general(left, right, (((1,), (1,)), ((), ())), preferred_element_type=F32)


def render_kernel(
    params_ref,
    cam_ref,
    eye_ref,
    camv_ref,
    eyev_ref,
    tile_ref,
    count_ref,
    fetch_ref,
    lists_ref,
    target_ref,
    rendered_ref,
    dense_ref,
    cams_ref,
    pv,
    pj,
    ask,
    req,
    rowsend,
    rowsin,
    stage,
    stage_hi,
    lhs,
    rhs,
    alphas,
    weights,
    lanes,
    gsend,
    gin,
    turned,
    spare_ask,
    spare_rows,
    spare_grads,
    cam_sem,
    par_sem,
    send_sems,
    recv_sems,
):
    me = lax.axis_index("space")
    view = lax.axis_index("view")
    other = 1 - view

    def blank():
        stage[...] = jnp.zeros(stage.shape, F32)
        stage_hi[...] = jnp.zeros(stage.shape, F32)

    def lay(first, stride, value):
        stage[pl.ds(first, TILES, stride=stride), :] = value[:, 0:128]
        stage_hi[pl.ds(first, TILES, stride=stride), :] = value[:, 128:256]

    def take(first, stride):
        rows = pl.ds(first, TILES, stride=stride)
        return jnp.concatenate([stage[rows, :], stage_hi[rows, :]], axis=1)

    def staged(rows=slice(None)):
        return jnp.concatenate([stage[rows, :], stage_hi[rows, :]], axis=1)

    barrier = pltpu.get_barrier_semaphore()

    def greet_own(d, c):
        pl.semaphore_signal(
            barrier, inc=1, device_id=(lax.rem(me + d, N), view), device_id_type=MESH
        )
        return c

    def greet_other(d, c):
        pl.semaphore_signal(
            barrier, inc=1, device_id=(lax.rem(me + d, N), other), device_id_type=MESH
        )
        return c

    lax.fori_loop(1, N, greet_own, 0)
    lax.fori_loop(0, N, greet_other, 0)

    loads = [
        pltpu.make_async_copy(
            params_ref.at[:, pl.ds(128 * b, 128)], pv.at[pl.ds(PITCH * b, ROWS)], par_sem.at[b]
        )
        for b in range(COLS)
    ]
    for load in loads:
        load.start()
    ask[...] = jnp.zeros(ask.shape, jnp.int32)
    ask[:, 0:CAP] = fetch_ref[...]
    cams_ref[0:8, :] = jnp.zeros((8, 128), F32)
    cams_ref[0:3, 0:4] = camv_ref[...]
    cams_ref[3:4, 0:3] = eyev_ref[...]
    rowsin[...] = jnp.zeros(rowsin.shape, F32)
    pl.semaphore_wait(barrier, 2 * N - 1)

    def push(src, dst, device, sems):
        return pltpu.make_async_remote_copy(
            src_ref=src,
            dst_ref=dst,
            send_sem=send_sems.at[sems],
            recv_sem=recv_sems.at[sems],
            device_id=device,
            device_id_type=MESH,
        )

    def exchange(src, dst, own, sems):
        def one(d, c):
            t = lax.rem(me + d, N)
            push(
                src.at[pl.ds(t, 1)],
                dst.at[pl.ds(me if own else N + me, 1)],
                (t, view if own else other),
                sems,
            ).start()
            return c

        lax.fori_loop(1 if own else 0, N, one, 0)

    def finish_send(src, own, sems):
        push(src, src, (me, view), sems).wait_send()

    def finish_recv(dst, own, sems):
        rows = pl.ds(0, N) if own else pl.ds(N, N)
        push(dst.at[rows], dst.at[rows], (me, view), sems).wait_recv()

    def keep(src, dst, spare, sems):
        mine = src.at[pl.ds(me, 1)]
        pltpu.make_async_copy(mine, dst.at[pl.ds(me, 1)], recv_sems.at[sems]).start()
        pltpu.make_async_copy(mine, spare, send_sems.at[sems]).start()

    exchange(ask, req, True, 0)
    keep(ask, req, spare_ask, 0)
    exchange(ask, req, False, 1)
    greeting = pltpu.make_async_remote_copy(
        src_ref=cams_ref.at[pl.ds(0, 8)],
        dst_ref=cams_ref.at[pl.ds(8, 8)],
        send_sem=cam_sem.at[0],
        recv_sem=cam_sem.at[1],
        device_id=(me, other),
        device_id_type=MESH,
    )
    greeting.start()

    for load in loads:
        load.wait()
    camera = [[cam_ref[r, c] for c in range(4)] for r in range(2)]
    eye = [eye_ref[0, c] for c in range(3)]
    values = [pv[pl.ds(p, COLS, stride=PITCH), :] for p in range(ROWS)]
    for f, row in enumerate(project(values, camera, eye)):
        pj[f] = row

    finish_recv(req, True, 0)
    wanted = jnp.concatenate([req[0:N, :], jnp.zeros((N, 128), jnp.int32)], axis=0).T[0:CAP, :]
    want_row, want_lane = wanted >> 7, wanted & 127

    def collect(f, c):
        stage[pl.ds(pl.multiple_of(f * CAP, CAP), CAP), :] = pick(pj[f], want_row, want_lane)
        return c

    lax.fori_loop(0, FEATS, collect, 0)
    rowsend[...] = stage[...].T[0:N, :]
    exchange(rowsend, rowsin, True, 2)
    keep(rowsend, rowsin, spare_rows, 2)

    finish_recv(req, False, 1)
    turned[...] = req[...].T[0:CAP, :]

    def locate(j, found):
        line = turned[pl.ds(j, 1), :]
        line_hi, line_lo = line >> 7, line & 127
        hit = iota((COLS, 128), 0) == jnp.broadcast_to(line_hi, (COLS, 128))
        spot = iota((COLS, 128), 1).astype(F32)
        digits = jnp.concatenate(
            [
                jnp.where(hit, j.astype(F32), 0.0),
                jnp.where(hit, spot, 0.0),
            ],
            axis=0,
        ).astype(BF16)
        ones = jnp.where(
            iota((128, 128), 0) == jnp.broadcast_to(line_lo, (128, 128)), 1.0, 0.0
        ).astype(BF16)
        return found + dot_nt(digits, ones)

    found = lax.fori_loop(0, CAP, locate, jnp.zeros((2 * COLS, 128), F32))
    found_row = found[0:COLS].astype(jnp.int32)
    found_lane = found[COLS : 2 * COLS].astype(jnp.int32)
    dense_ref[FEATS] = jnp.where(found_lane < N, 1.0, 0.0)

    pixel = iota((TILES, PX), 1)
    u = (pixel % 16).astype(F32) - 7.5
    w = (pixel // 16).astype(F32) - 7.5
    basis = [jnp.ones_like(u), u, w, u * u, u * w, w * w]
    blank()
    for c in range(6):
        for part in range(3):
            lay(3 * c + part, GROUP, basis[c])
    rhs[...] = staged().astype(BF16)

    entry_own = lists_ref[...] >> 4
    entry_pos = lists_ref[...] & 15
    finish_recv(rowsin, True, 2)
    stage[...] = rowsin[...].T

    entries = []
    for f in range(FEATS):
        table = stage[CAP * f : CAP * (f + 1), :]
        entries.append(
            jnp.concatenate(
                [
                    pick(table, entry_pos[:, h : h + 128], entry_own[:, h : h + 128])
                    for h in (0, 128)
                ],
                axis=1,
            )
        )

    tile_row = iota((TILES, PX), 0)
    mid_x = jnp.zeros((TILES, PX), F32)
    mid_y = jnp.zeros((TILES, PX), F32)
    live = jnp.zeros((TILES, PX), jnp.int32)
    for t in range(TILES):
        here = tile_row == t
        mid_x = jnp.where(here, (tile_ref[0, t] % 32 * 16 + 8).astype(F32), mid_x)
        mid_y = jnp.where(here, (tile_ref[0, t] // 32 * 16 + 8).astype(F32), mid_y)
        live = jnp.where(here, count_ref[0, t], live)
    alive = pixel < live
    spot_x = entries[0] * 512.0 - mid_x
    spot_y = entries[1] * 512.0 - mid_y
    con_a, con_b, con_c = [entries[2 + i] * (1.0 / 262144.0) for i in range(3)]
    lin_x = con_a * spot_x + con_b * spot_y
    lin_y = con_c * spot_y + con_b * spot_x
    level = entries[5] - 0.5 * (spot_x * lin_x + spot_y * lin_y)
    coeffs = [level, lin_x, lin_y, -0.5 * con_a, -con_b, -0.5 * con_c]
    blank()
    for c in range(6):
        coeff = jnp.where(alive, coeffs[c] * LOG2E, -1e30 if c == 0 else 0.0)
        for part, piece in enumerate(split(coeff, 3)):
            lay(3 * c + part, GROUP, piece)
    colours = [jnp.where(alive, entries[6 + c], 0.0) for c in range(3)]
    for c in range(3):
        high, low = split(colours[c], 2)
        for part, piece in enumerate((high, high, low)):
            lay(18 + 3 * c + part, GROUP, piece)
        lay(27 + c, GROUP, colours[c])
    lanes[...] = staged().T

    group_mask = iota((TILES, TILES * GROUP), 1) // GROUP == iota((TILES, TILES * GROUP), 0)

    def forward(step, carry):
        through, images = carry[0], list(carry[1:])
        first = pl.multiple_of(step * CHUNK, CHUNK)
        rows = pl.ds(pl.multiple_of(step * CHUNK * TILES, CHUNK * TILES), CHUNK * TILES)
        spread = jnp.where(
            group_mask[None], lanes[pl.ds(first, CHUNK), :][:, None, :], 0.0
        ).reshape(CHUNK * TILES, TILES * GROUP)
        low = spread.astype(BF16)
        lhs[rows, :] = low
        power = jnp.dot(low, rhs[...], preferred_element_type=F32)
        alpha_all = jnp.exp2(power)
        for i in range(CHUNK):
            alpha = alpha_all[i * TILES : (i + 1) * TILES]
            weight = through * alpha
            through = through - weight
            at = pl.ds(pl.multiple_of((first + i) * TILES, TILES), TILES)
            alphas[at, :] = alpha
            weights[at, :] = weight
            group = spread[i * TILES : (i + 1) * TILES]
            for c in range(3):
                line = jnp.sum(
                    jnp.where(iota((TILES, TILES * GROUP), 1) % GROUP == 27 + c, group, 0.0),
                    axis=1,
                    keepdims=True,
                )
                images[c] = images[c] + weight * line
        return (through, *images)

    zero = jnp.zeros((TILES, PX), F32)
    _, *images = lax.fori_loop(0, K // CHUNK, forward, (jnp.ones((TILES, PX), F32), zero, zero, zero))

    blank()
    shades = []
    for c in range(3):
        rendered_ref[:, c, :] = images[c]
        shade = (images[c] - target_ref[:, c, :]) * (1.0 / 256.0)
        high, low = split(shade, 2)
        shades.append(split(shade, 3))
        for part, piece in enumerate((high, low, high)):
            lay(18 + 3 * c + part, GROUP, piece)
    rhs[...] = staged().astype(BF16)
    blank()
    for c in range(6):
        lay(c, MOMS, basis[c])
    for c in range(3):
        for part in range(3):
            lay(128 + 6 + 3 * c + part, MOMS, shades[c][part])
    moment_rows = staged(slice(0, 128)).astype(BF16)
    shade_rows = staged(slice(128, 256)).astype(BF16)
    moment_mask = iota((TILES, 128), 1) // MOMS == iota((TILES, 128), 0)

    def backward(back, behind):
        step = K // CHUNK - 1 - back
        first = pl.multiple_of(step * CHUNK, CHUNK)
        rows = pl.ds(pl.multiple_of(step * CHUNK * TILES, CHUNK * TILES), CHUNK * TILES)
        tone = jnp.dot(lhs[rows, :], rhs[...], preferred_element_type=F32)
        alpha = alphas[rows, :]
        weight = weights[rows, :]
        slopes = [None] * CHUNK
        for i in reversed(range(CHUNK)):
            at = slice(i * TILES, (i + 1) * TILES)
            gap = tone[at] - behind
            slopes[i] = weight[at] * gap
            behind = behind + alpha[at] * gap
        slope = jnp.concatenate(slopes, axis=0)
        total = jnp.zeros((CHUNK * TILES, 128), F32)
        for piece in split_low(slope, 3):
            total = total + dot_nt(piece, moment_rows)
        for piece in split_low(weight, 2):
            total = total + dot_nt(piece, shade_rows)
        total = jnp.where(moment_mask[None], total.reshape(CHUNK, TILES, 128), 0.0)
        lanes[pl.ds(first, CHUNK), 0:128] = jnp.sum(total, axis=1)
        return behind

    lax.fori_loop(0, K // CHUNK, backward, zero)

    turned_sums = lanes[:, 0:128].T
    stage[0:128, :] = turned_sums[:, 0:128]
    stage_hi[0:128, :] = turned_sums[:, 128:256]
    sums = [take(c, MOMS) for c in range(15)]
    s_1, s_u, s_w, s_uu, s_uw, s_ww = sums[0:6]
    d_x = s_u - spot_x * s_1
    d_y = s_w - spot_y * s_1
    d_xx = s_uu - 2.0 * spot_x * s_u + spot_x * spot_x * s_1
    d_yy = s_ww - 2.0 * spot_y * s_w + spot_y * spot_y * s_1
    d_xy = s_uw - spot_x * s_w - spot_y * s_u + spot_x * spot_y * s_1
    slopes = [
        512.0 * (con_a * d_x + con_b * d_y),
        512.0 * (con_c * d_y + con_b * d_x),
        d_xx * (-0.5 / 262144.0),
        d_xy * (-1.0 / 262144.0),
        d_yy * (-0.5 / 262144.0),
        s_1,
        *[sums[6 + 3 * c] + sums[7 + 3 * c] + sums[8 + 3 * c] for c in range(3)],
    ]
    blank()
    for f in range(FEATS):
        for part, piece in enumerate(split(jnp.where(alive, slopes[f], 0.0), 3)):
            lay(FEATS * part + f, GROUP, piece)

    def gather_up(t, total):
        listed = lists_ref[pl.ds(t, 1), :]
        block = staged(pl.ds(pl.multiple_of(t * GROUP, GROUP), GROUP))
        at_pos = iota((CAP, K), 0) == jnp.broadcast_to(listed & 15, (CAP, K))
        left = jnp.where(at_pos[None], block[0 : 3 * FEATS][:, None, :], 0.0)
        left = left.reshape(3 * FEATS * CAP, K).astype(BF16)
        at_own = iota((N, K), 0) == jnp.broadcast_to(listed >> 4, (N, K))
        return total + dot_nt(left, jnp.where(at_own, 1.0, 0.0).astype(BF16))

    total = lax.fori_loop(0, TILES, gather_up, jnp.zeros((3 * FEATS * CAP, N), F32))
    size = FEATS * CAP
    summed = total[0:size] + total[size : 2 * size] + total[2 * size : 3 * size]
    gsend[...] = jnp.zeros(gsend.shape, F32)
    gsend[:, 0:size] = summed.T

    exchange(gsend, gin, True, 3)
    keep(gsend, gin, spare_grads, 3)
    exchange(gsend, gin, False, 4)
    finish_recv(gin, True, 3)
    finish_recv(gin, False, 4)
    stage[...] = gin[...].T

    def place(f, c):
        dense_ref[f] = pick(
            stage[pl.ds(pl.multiple_of(f * CAP, CAP), CAP), :], found_row, found_lane
        )
        return c

    lax.fori_loop(0, FEATS, place, 0)

    finish_send(ask, True, 0)
    finish_send(ask, False, 1)
    finish_send(rowsend, True, 2)
    finish_send(gsend, True, 3)
    finish_send(gsend, False, 4)
    greeting.wait()


def owner_kernel(params_ref, dense_ref, cams_ref, grads_ref, pv, gv, in_sem, out_sem):
    loads = [
        pltpu.make_async_copy(
            params_ref.at[:, pl.ds(128 * b, 128)], pv.at[pl.ds(PITCH * b, ROWS)], in_sem.at[b]
        )
        for b in range(COLS)
    ]
    for load in loads:
        load.start()
    own = dense_ref[FEATS] > 0.5

    def chosen(row, col):
        return jnp.where(
            own,
            jnp.broadcast_to(cams_ref[row : row + 1, col : col + 1], own.shape),
            jnp.broadcast_to(cams_ref[8 + row : 9 + row, col : col + 1], own.shape),
        )

    camera = [[chosen(r, c) for c in range(4)] for r in range(2)]
    eye = [chosen(3, c) for c in range(3)]
    for load in loads:
        load.wait()
    values = [pv[pl.ds(p, COLS, stride=PITCH), :] for p in range(ROWS)]
    _, pull = jax.vjp(lambda rows: project(rows, camera, eye), values)
    (grads,) = pull([dense_ref[f] for f in range(FEATS)])
    for p in range(ROWS):
        gv[pl.ds(p, COLS, stride=PITCH), :] = grads[p]
    stores = [
        pltpu.make_async_copy(
            gv.at[pl.ds(PITCH * b, ROWS)], grads_ref.at[:, pl.ds(128 * b, 128)], out_sem.at[b]
        )
        for b in range(COLS)
    ]
    for store in stores:
        store.start()
    for store in stores:
        store.wait()


def on_device(params, camera, eye_point, tile_of, fetch, lists, counts, target):
    vmem = pl.BlockSpec(memory_space=pltpu.VMEM)
    smem = pl.BlockSpec(memory_space=pltpu.SMEM)
    hbm = pl.BlockSpec(memory_space=pl.ANY)
    rendered, dense, cams = pl.pallas_call(
        render_kernel,
        out_shape=(
            jax.ShapeDtypeStruct((TILES, 3, PX), F32),
            jax.ShapeDtypeStruct((FEATS + 1, COLS, 128), F32),
            jax.ShapeDtypeStruct((16, 128), F32),
        ),
        in_specs=[hbm, smem, smem, vmem, vmem, smem, smem, vmem, vmem, vmem],
        out_specs=(vmem, vmem, vmem),
        scratch_shapes=[
            pltpu.VMEM((COLS * PITCH, 128), F32),
            pltpu.VMEM((FEATS, COLS, 128), F32),
            pltpu.VMEM((N, 128), jnp.int32),
            pltpu.VMEM((2 * N, 128), jnp.int32),
            pltpu.VMEM((N, 256), F32),
            pltpu.VMEM((2 * N, 256), F32),
            pltpu.VMEM((256, 128), F32),
            pltpu.VMEM((256, 128), F32),
            pltpu.VMEM((K * TILES, 256), BF16),
            pltpu.VMEM((256, PX), BF16),
            pltpu.VMEM((K * TILES, PX), F32),
            pltpu.VMEM((K * TILES, PX), F32),
            pltpu.VMEM((K, 256), F32),
            pltpu.VMEM((N, 256), F32),
            pltpu.VMEM((2 * N, 256), F32),
            pltpu.VMEM((CAP, 128), jnp.int32),
            pltpu.VMEM((1, 128), jnp.int32),
            pltpu.VMEM((1, 256), F32),
            pltpu.VMEM((1, 256), F32),
            pltpu.SemaphoreType.DMA((2,)),
            pltpu.SemaphoreType.DMA((COLS,)),
            pltpu.SemaphoreType.DMA((5,)),
            pltpu.SemaphoreType.DMA((5,)),
        ],
        compiler_params=pltpu.CompilerParams(
            collective_id=0, has_side_effects=True, vmem_limit_bytes=40 << 20
        ),
        name="render",
    )(
        params,
        camera[0],
        eye_point,
        camera[0],
        eye_point,
        tile_of,
        counts,
        fetch[0, 0],
        lists[0],
        target[0],
    )
    grads = pl.pallas_call(
        owner_kernel,
        out_shape=jax.ShapeDtypeStruct(params.shape, F32),
        in_specs=[hbm, vmem, vmem],
        out_specs=hbm,
        scratch_shapes=[
            pltpu.VMEM((COLS * PITCH, 128), F32),
            pltpu.VMEM((COLS * PITCH, 128), F32),
            pltpu.SemaphoreType.DMA((COLS,)),
            pltpu.SemaphoreType.DMA((COLS,)),
        ],
        compiler_params=pltpu.CompilerParams(vmem_limit_bytes=32 << 20),
        name="owner",
    )(params, dense, cams)
    return (rendered[None], grads)


def solution(mesh):
    placed = (
        P(None, "space"),
        P("view", None, None),
        P("view", None),
        P("view", "space"),
        P("view", "space", None, None),
        P("view", "space", None),
        P("view", "space"),
        P("view", "space", None, None),
    )
    return jax.shard_map(
        on_device,
        mesh=mesh,
        in_specs=placed,
        out_specs=(P("view", "space", None, None), P(None, "space")),
        check_vma=False,
    )
```

time: 683 us -> 49 us (0.07)
  waiting for transfers between devices: 465 us -> 0 us
  other arithmetic: 94.5 us -> 0 us
  local copies, waits for them, and re-layouts: 93.4 us -> 3.81 us
  Pallas kernels: 0 us -> 44.3 us
  between operations: 18 us -> 0.69 us
  matrix products: 10.1 us -> 0 us
    reduce_scatter x1 -> x0, waiting for transfers between devices: 322 us -> none  [on_device(): lax.psum_scatter(dense, 'space', scatter_dimension=1, tiled=True)]
    all_gather x1 -> x0, waiting for transfers between devices: 78.1 us -> none  [on_device(): everything = lax.all_gather(projected, 'space', axis=1, tiled=True)]
    psum x1 -> x0, waiting for transfers between devices: 64.6 us -> none  [on_device(): summed = lax.psum(param_grad, 'view')]
    scatter-add x4 -> x0, other arithmetic: 57.8 us -> none  [the longest x3 46.1 us: on_device(): jnp.zeros((9, owners * shard_len), jnp.float32).at[:, flat_ids]]
    pallas_call x0 -> x2, Pallas kernels: none -> 44.3 us  [the longest x1 42.2 us: on_device(): pl.pallas_call(render_kernel, out_shape=(jax.ShapeDtypeStruct((TILES, 3,...]
    scatter-add x2 -> x0, local copies, waits for them, and re-layouts: 36.9 us -> none  [on_device(): jnp.zeros((9, owners * shard_len), jnp.float32).at[:, flat_ids]]
    all_gather x1 -> x0, local copies, waits for them, and re-layouts: 31.5 us -> none  [on_device(): everything = lax.all_gather(projected, 'space', axis=1, tiled=True)]
    gather x3 -> x0, local copies, waits for them, and re-layouts: 16.3 us -> none  [the longest x1 10.5 us: on_device(): sectioning = everything[:, flat_ids]]
  transfers between devices with their start and end apart: 3 -> 0, of which waited for: 3 -> 0; matrix products, arithmetic and copies ran while one was open for 1% -> 0% of each run, Pallas kernels for 0% -> 0%
where the time goes in v1:
time: 49 us; the launch traced here: 48.8 us
  Pallas kernels  44.3 us (90%)
  local copies, waits for them, and re-layouts  3.81 us (8%)
  between operations  0.69 us (1%)
    pallas_call x1, Pallas kernels, on_device(): pl.pallas_call(render_kernel, out_shape=(jax.ShapeDtypeStruct((TILES, 3,...  42.2 us
    unnamed x18, local copies, waits for them, and re-layouts  3.81 us
    pallas_call x1, Pallas kernels, on_device(): pl.pallas_call(owner_kernel, out_shape=jax.ShapeDtypeStruct(params.shape,...  2.11 us

profile of v1, /device:TPU:1, one launch (start us, length us, event | category | flops | bytes accessed | tf_op | source)
XLA Modules:
  0.0 48.8 jit_solution(799364386742914726)
XLA Ops:
  0.6 0.0 copy-start.6
  0.6 0.7 %copy-done.6 = f32[1,3,4]{2,0,1:T(1,128)S(1)} copy-done((f32[1,3,4]{2,0,1:T(1,128)S(1)}, f32[1,3,4]{2,0,1:T(1,128)}, u32[]{:S(2)}) %copy-start.6) | copy-done | bytes 72
  1.3 0.0 copy-start.5
  1.3 0.8 %copy.10 = s32[1,1,64,16]{3,2,1,0:T(8,128)S(1)} copy(s32[1,1,64,16]{2,3,1,0:T(8,128)} %param.12) | data formatting | bytes 8192 | tf_op args[4]
  2.1 0.0 copy-done.5
  2.1 0.0 copy-start.1
  2.1 0.0 copy-start.2
  2.2 0.0 copy-start.3
  2.2 0.0 copy-start.4
  2.2 0.6 %copy-done.1 = s32[1,8,256]{2,1,0:T(8,128)S(1)} copy-done((s32[1,8,256]{2,1,0:T(8,128)S(1)}, s32[1,8,256]{2,1,0:T(8,128)}, u32[]{:S(2)}) %copy-start.1) | copy-done | bytes 8216
  2.8 0.0 copy-done.2
  2.8 0.0 copy-done.3
  2.8 0.0 copy-done.4
  2.8 0.0 copy-start
  2.8 1.0 %copy-done = f32[59,2048]{1,0:T(8,128)S(1)} copy-done((f32[59,2048]{1,0:T(8,128)S(1)}, f32[59,2048]{1,0:T(8,128)}, u32[]{:S(2)}) %copy-start) | copy-done | bytes 483352
  3.9 42.2 %render.1 = (f32[8,3,256]{2,1,0:T(4,128)S(1)}, f32[10,16,128]{2,1,0:T(8,128)S(1)}, f32[16,128]{1,0:T(8,128)S(1)}) custom-call(f32[59,2048]{1,0:T(8,128)S(1)} %copy-done, f32[3,4]{1,0:T(4,128)S(1)} %bitcast.12, f32[1,3]{1,0:T(1,128)S(1)} %copy-done.2, f32[3,4]{1,0:T(4,128)S(1)} %bitcast.13, f32[1,3]{1,0:T(1,128)S(1)} %copy-done.2, s32[1,8]{1,0:T(1,128)S(1)} %copy-done.3, ...), custom_call_target="tpu_custom_call" | custom-call | tf_op jit(solution)/shard_map/render/pallas_call | solution.py:595
  46.0 0.6 %copy.12 = f32[1,8,3,256]{3,1,2,0:T(8,128)} copy(f32[1,8,3,256]{3,2,1,0:T(4,128)S(1)} %bitcast.11) | data formatting | bytes 49152
  46.6 2.1 %owner.1 = f32[59,2048]{1,0:T(8,128)} custom-call(f32[59,2048]{1,0:T(8,128)S(1)} %copy-done, f32[10,16,128]{2,1,0:T(8,128)S(1)} %get-tuple-element.6.dense_ref, f32[16,128]{1,0:T(8,128)S(1)} %get-tuple-element.7.cams_ref), custom_call_target="tpu_custom_call" | custom-call | tf_op jit(solution)/shard_map/owner/pallas_call | solution.py:645
  (2 shorter events, 0.0 us)
Async XLA Ops:
  0.6 0.7 %copy-start.6 = (f32[1,3,4]{2,0,1:T(1,128)S(1)}, f32[1,3,4]{2,0,1:T(1,128)}, u32[]{:S(2)}) copy-start(f32[1,3,4]{2,0,1:T(1,128)} %param.9) | copy-start | bytes 148
  1.3 0.8 %copy-start.5 = (f32[1,8,3,256]{3,1,2,0:T(8,128)S(1)}, f32[1,8,3,256]{3,1,2,0:T(8,128)}, u32[]{:S(2)}) copy-start(f32[1,8,3,256]{3,1,2,0:T(8,128)} %param.15) | copy-start | bytes 73732
  2.1 0.7 %copy-start.1 = (s32[1,8,256]{2,1,0:T(8,128)S(1)}, s32[1,8,256]{2,1,0:T(8,128)}, u32[]{:S(2)}) copy-start(s32[1,8,256]{2,1,0:T(8,128)} %param.13) | copy-start | bytes 24580
  2.1 0.7 %copy-start.2 = (f32[1,3]{1,0:T(1,128)S(1)}, f32[1,3]{1,0:T(1,128)}, u32[]{:S(2)}) copy-start(f32[1,3]{1,0:T(1,128)} %eyev_ref.1) | copy-start | bytes 40
  2.2 0.7 %copy-start.3 = (s32[1,8]{1,0:T(1,128)S(1)}, s32[1,8]{1,0:T(1,128)}, u32[]{:S(2)}) copy-start(s32[1,8]{1,0:T(1,128)} %tile_ref.1) | copy-start | bytes 100
  2.2 0.7 %copy-start.4 = (s32[1,8]{1,0:T(1,128)S(1)}, s32[1,8]{1,0:T(1,128)}, u32[]{:S(2)}) copy-start(s32[1,8]{1,0:T(1,128)} %count_ref.1) | copy-start | bytes 100
  2.8 1.0 %copy-start = (f32[59,2048]{1,0:T(8,128)S(1)}, f32[59,2048]{1,0:T(8,128)}, u32[]{:S(2)}) copy-start(f32[59,2048]{1,0:T(8,128)} %params_ref.3) | copy-start | bytes 1449988

commit v2 on v1

--- a/solution.py
+++ b/solution.py
@@ -43,6 +43,8 @@
 GROUP = 32
 MOMS = 16
 CHUNK = 32
+UNROLL_F = 8
+UNROLL_B = 8
 
 
 def harmonics(dir_x, dir_y, dir_z):
@@ -157,7 +159,7 @@
 def pick(table, row, lane):
     shape = row.shape
     found = jnp.zeros(shape, F32)
-    for r in range(16):
+    for r in range(table.shape[0]):
         line = jnp.broadcast_to(table[r : r + 1, :], shape)
         found = jnp.where(row == r, jnp.take_along_axis(line, lane, axis=1), found)
     return found
@@ -168,19 +170,24 @@
 
 
 def render_kernel(
-    params_ref,
+    params_hbm,
+    cam_hbm,
+    eye_hbm,
+    tile_hbm,
+    count_hbm,
+    fetch_hbm,
+    lists_hbm,
+    target_hbm,
+    rendered_ref,
+    dense_ref,
+    cams_ref,
     cam_ref,
     eye_ref,
-    camv_ref,
-    eyev_ref,
     tile_ref,
     count_ref,
     fetch_ref,
     lists_ref,
     target_ref,
-    rendered_ref,
-    dense_ref,
-    cams_ref,
     pv,
     pj,
     ask,
@@ -200,6 +207,9 @@
     spare_ask,
     spare_rows,
     spare_grads,
+    pos_ones,
+    own_ones,
+    in_sems,
     cam_sem,
     par_sem,
     send_sems,
@@ -224,38 +234,44 @@
     def staged(rows=slice(None)):
         return jnp.concatenate([stage[rows, :], stage_hi[rows, :]], axis=1)
 
+    small = [
+        pltpu.make_async_copy(src, dst, in_sems.at[i])
+        for i, (src, dst) in enumerate(
+            [
+                (fetch_hbm, fetch_ref),
+                (cam_hbm, cam_ref),
+                (eye_hbm, eye_ref),
+                (tile_hbm, tile_ref),
+                (count_hbm, count_ref),
+                (lists_hbm, lists_ref),
+                (target_hbm, target_ref),
+            ]
+        )
+    ]
+    small[0].start()
     barrier = pltpu.get_barrier_semaphore()
-
-    def greet_own(d, c):
+    pl.semaphore_signal(barrier, inc=1, device_id=(me, other), device_id_type=MESH)
+
+    def greet(d, c):
         pl.semaphore_signal(
             barrier, inc=1, device_id=(lax.rem(me + d, N), view), device_id_type=MESH
         )
         return c
 
-    def greet_other(d, c):
-        pl.semaphore_signal(
-            barrier, inc=1, device_id=(lax.rem(me + d, N), other), device_id_type=MESH
-        )
-        return c
-
-    lax.fori_loop(1, N, greet_own, 0)
-    lax.fori_loop(0, N, greet_other, 0)
-
+    lax.fori_loop(1, N, greet, 0, unroll=7)
     loads = [
         pltpu.make_async_copy(
-            params_ref.at[:, pl.ds(128 * b, 128)], pv.at[pl.ds(PITCH * b, ROWS)], par_sem.at[b]
+            params_hbm.at[:, pl.ds(128 * b, 128)], pv.at[pl.ds(PITCH * b, ROWS)], par_sem.at[b]
         )
         for b in range(COLS)
     ]
-    for load in loads:
+    for load in [*small[1:], *loads]:
         load.start()
     ask[...] = jnp.zeros(ask.shape, jnp.int32)
-    ask[:, 0:CAP] = fetch_ref[...]
-    cams_ref[0:8, :] = jnp.zeros((8, 128), F32)
-    cams_ref[0:3, 0:4] = camv_ref[...]
-    cams_ref[3:4, 0:3] = eyev_ref[...]
     rowsin[...] = jnp.zeros(rowsin.shape, F32)
-    pl.semaphore_wait(barrier, 2 * N - 1)
+    small[0].wait()
+    ask[:, 0:CAP] = fetch_ref[...].T
+    pl.semaphore_wait(barrier, N)
 
     def push(src, dst, device, sems):
         return pltpu.make_async_remote_copy(
@@ -278,7 +294,7 @@
             ).start()
             return c
 
-        lax.fori_loop(1 if own else 0, N, one, 0)
+        lax.fori_loop(1 if own else 0, N, one, 0, unroll=7 if own else 8)
 
     def finish_send(src, own, sems):
         push(src, src, (me, view), sems).wait_send()
@@ -294,7 +310,21 @@
 
     exchange(ask, req, True, 0)
     keep(ask, req, spare_ask, 0)
-    exchange(ask, req, False, 1)
+    for load in [*small[1:], *loads]:
+        load.wait()
+    camera = [[cam_ref[r, 0, c] for c in range(4)] for r in range(2)]
+    eye = [eye_ref[0, c] for c in range(3)]
+    values = [pv[pl.ds(p, COLS, stride=PITCH), :] for p in range(ROWS)]
+    for f, row in enumerate(project(values, camera, eye)):
+        pj[f] = row
+
+    sheet = jnp.zeros((8, 128), F32)
+    spots = [(r, c, camera[r][c]) for r in range(2) for c in range(4)]
+    spots += [(3, c, eye[c]) for c in range(3)]
+    for r, c, number in spots:
+        here = (iota((8, 128), 0) == r) & (iota((8, 128), 1) == c)
+        sheet = jnp.where(here, number, sheet)
+    cams_ref[0:8, :] = sheet
     greeting = pltpu.make_async_remote_copy(
         src_ref=cams_ref.at[pl.ds(0, 8)],
         dst_ref=cams_ref.at[pl.ds(8, 8)],
@@ -305,28 +335,29 @@
     )
     greeting.start()
 
-    for load in loads:
-        load.wait()
-    camera = [[cam_ref[r, c] for c in range(4)] for r in range(2)]
-    eye = [eye_ref[0, c] for c in range(3)]
-    values = [pv[pl.ds(p, COLS, stride=PITCH), :] for p in range(ROWS)]
-    for f, row in enumerate(project(values, camera, eye)):
-        pj[f] = row
-
     finish_recv(req, True, 0)
-    wanted = jnp.concatenate([req[0:N, :], jnp.zeros((N, 128), jnp.int32)], axis=0).T[0:CAP, :]
+    wanted = req[0:N, :].T[0:CAP, :]
+    wanted = jnp.concatenate([wanted[0:8], wanted[8:16]], axis=1)
     want_row, want_lane = wanted >> 7, wanted & 127
-
-    def collect(f, c):
-        stage[pl.ds(pl.multiple_of(f * CAP, CAP), CAP), :] = pick(pj[f], want_row, want_lane)
-        return c
-
-    lax.fori_loop(0, FEATS, collect, 0)
+    for f in range(FEATS):
+        found = pick(pj[f], want_row, want_lane)
+        stage[CAP * f : CAP * f + 8, :] = found
+        stage[CAP * f + 8 : CAP * (f + 1), :] = pltpu.roll(found, N, 1)
     rowsend[...] = stage[...].T[0:N, :]
     exchange(rowsend, rowsin, True, 2)
     keep(rowsend, rowsin, spare_rows, 2)
 
-    finish_recv(req, False, 1)
+    passed = pltpu.make_async_remote_copy(
+        src_ref=req.at[pl.ds(0, N)],
+        dst_ref=req.at[pl.ds(N, N)],
+        send_sem=send_sems.at[1],
+        recv_sem=recv_sems.at[1],
+        device_id=(me, other),
+        device_id_type=MESH,
+    )
+    passed.start()
+
+    passed.wait_recv()
     turned[...] = req[...].T[0:CAP, :]
 
     def locate(j, found):
@@ -361,18 +392,27 @@
             lay(3 * c + part, GROUP, basis[c])
     rhs[...] = staged().astype(BF16)
 
-    entry_own = lists_ref[...] >> 4
-    entry_pos = lists_ref[...] & 15
+    for t in range(TILES):
+        listed = lists_ref[t : t + 1, :]
+        at_pos = iota((CAP, K), 0) == jnp.broadcast_to(listed & 15, (CAP, K))
+        at_own = iota((N, K), 0) == jnp.broadcast_to(listed >> 4, (N, K))
+        pos_ones[t] = jnp.where(at_pos, 1.0, 0.0).astype(BF16)
+        own_ones[t] = jnp.where(at_own, 1.0, 0.0).astype(BF16)
+
+    entry_row = lists_ref[...] & 7
+    entry_lane = (lists_ref[...] >> 4) + ((lists_ref[...] & 8) << 3)
     finish_recv(rowsin, True, 2)
     stage[...] = rowsin[...].T
 
     entries = []
     for f in range(FEATS):
-        table = stage[CAP * f : CAP * (f + 1), :]
+        first_half = stage[CAP * f : CAP * f + 8, :]
+        second_half = stage[CAP * f + 8 : CAP * (f + 1), :]
+        table = jnp.where(iota((8, 128), 1) < N, first_half, pltpu.roll(second_half, N, 1))
         entries.append(
             jnp.concatenate(
                 [
-                    pick(table, entry_pos[:, h : h + 128], entry_own[:, h : h + 128])
+                    pick(table, entry_row[:, h : h + 128], entry_lane[:, h : h + 128])
                     for h in (0, 128)
                 ],
                 axis=1,
@@ -403,12 +443,16 @@
             lay(3 * c + part, GROUP, piece)
     colours = [jnp.where(alive, entries[6 + c], 0.0) for c in range(3)]
     for c in range(3):
-        high, low = split(colours[c], 2)
+        high, low, rest = split(colours[c], 3)
         for part, piece in enumerate((high, high, low)):
             lay(18 + 3 * c + part, GROUP, piece)
-        lay(27 + c, GROUP, colours[c])
+        lay(27 + c, GROUP, rest)
     lanes[...] = staged().T
 
+    column = iota((TILES * GROUP, 128), 0) % GROUP
+    wants = iota((TILES * GROUP, 128), 1)
+    adds = (column == 18 + 3 * wants) | (column == 20 + 3 * wants) | (column == 27 + wants)
+    chooser = jnp.where(adds & (wants < 3), 1.0, 0.0).astype(BF16)
     group_mask = iota((TILES, TILES * GROUP), 1) // GROUP == iota((TILES, TILES * GROUP), 0)
 
     def forward(step, carry):
@@ -421,32 +465,28 @@
         low = spread.astype(BF16)
         lhs[rows, :] = low
         power = jnp.dot(low, rhs[...], preferred_element_type=F32)
+        paint = jnp.dot(low, chooser, preferred_element_type=F32)
         alpha_all = jnp.exp2(power)
+        alphas[rows, :] = alpha_all
         for i in range(CHUNK):
             alpha = alpha_all[i * TILES : (i + 1) * TILES]
             weight = through * alpha
-            through = through - weight
+            through = through * (1.0 - alpha)
             at = pl.ds(pl.multiple_of((first + i) * TILES, TILES), TILES)
-            alphas[at, :] = alpha
             weights[at, :] = weight
-            group = spread[i * TILES : (i + 1) * TILES]
             for c in range(3):
-                line = jnp.sum(
-                    jnp.where(iota((TILES, TILES * GROUP), 1) % GROUP == 27 + c, group, 0.0),
-                    axis=1,
-                    keepdims=True,
-                )
-                images[c] = images[c] + weight * line
+                shine = paint[i * TILES : (i + 1) * TILES, c : c + 1]
+                images[c] = images[c] + weight * shine
         return (through, *images)
 
     zero = jnp.zeros((TILES, PX), F32)
-    _, *images = lax.fori_loop(0, K // CHUNK, forward, (jnp.ones((TILES, PX), F32), zero, zero, zero))
+    _, *images = lax.fori_loop(0, K // CHUNK, forward, (jnp.ones((TILES, PX), F32), zero, zero, zero), unroll=UNROLL_F)
 
     blank()
     shades = []
     for c in range(3):
-        rendered_ref[:, c, :] = images[c]
-        shade = (images[c] - target_ref[:, c, :]) * (1.0 / 256.0)
+        rendered_ref[c] = images[c]
+        shade = (images[c] - target_ref[c]) * (1.0 / 256.0)
         high, low = split(shade, 2)
         shades.append(split(shade, 3))
         for part, piece in enumerate((high, low, high)):
@@ -474,10 +514,10 @@
             at = slice(i * TILES, (i + 1) * TILES)
             gap = tone[at] - behind
             slopes[i] = weight[at] * gap
-            behind = behind + alpha[at] * gap
+            behind = behind * (1.0 - alpha[at]) + alpha[at] * tone[at]
         slope = jnp.concatenate(slopes, axis=0)
         total = jnp.zeros((CHUNK * TILES, 128), F32)
-        for piece in split_low(slope, 3):
+        for piece in split_low(slope, 2):
             total = total + dot_nt(piece, moment_rows)
         for piece in split_low(weight, 2):
             total = total + dot_nt(piece, shade_rows)
@@ -485,7 +525,7 @@
         lanes[pl.ds(first, CHUNK), 0:128] = jnp.sum(total, axis=1)
         return behind
 
-    lax.fori_loop(0, K // CHUNK, backward, zero)
+    lax.fori_loop(0, K // CHUNK, backward, zero, unroll=UNROLL_B)
 
     turned_sums = lanes[:, 0:128].T
     stage[0:128, :] = turned_sums[:, 0:128]
@@ -508,21 +548,16 @@
     ]
     blank()
     for f in range(FEATS):
-        for part, piece in enumerate(split(jnp.where(alive, slopes[f], 0.0), 3)):
+        for part, piece in enumerate(split(jnp.where(alive, slopes[f], 0.0), 2)):
             lay(FEATS * part + f, GROUP, piece)
 
-    def gather_up(t, total):
-        listed = lists_ref[pl.ds(t, 1), :]
-        block = staged(pl.ds(pl.multiple_of(t * GROUP, GROUP), GROUP))
-        at_pos = iota((CAP, K), 0) == jnp.broadcast_to(listed & 15, (CAP, K))
-        left = jnp.where(at_pos[None], block[0 : 3 * FEATS][:, None, :], 0.0)
-        left = left.reshape(3 * FEATS * CAP, K).astype(BF16)
-        at_own = iota((N, K), 0) == jnp.broadcast_to(listed >> 4, (N, K))
-        return total + dot_nt(left, jnp.where(at_own, 1.0, 0.0).astype(BF16))
-
-    total = lax.fori_loop(0, TILES, gather_up, jnp.zeros((3 * FEATS * CAP, N), F32))
+    total = jnp.zeros((2 * FEATS * CAP, N), F32)
+    for t in range(TILES):
+        block = staged(slice(t * GROUP, t * GROUP + 2 * FEATS)).astype(BF16)
+        left = block[:, None, :] * pos_ones[t][None]
+        total = total + dot_nt(left.reshape(2 * FEATS * CAP, K), own_ones[t])
     size = FEATS * CAP
-    summed = total[0:size] + total[size : 2 * size] + total[2 * size : 3 * size]
+    summed = total[0:size] + total[size : 2 * size]
     gsend[...] = jnp.zeros(gsend.shape, F32)
     gsend[:, 0:size] = summed.T
 
@@ -533,23 +568,21 @@
     finish_recv(gin, False, 4)
     stage[...] = gin[...].T
 
-    def place(f, c):
-        dense_ref[f] = pick(
-            stage[pl.ds(pl.multiple_of(f * CAP, CAP), CAP), :], found_row, found_lane
-        )
-        return c
-
-    lax.fori_loop(0, FEATS, place, 0)
+    for f in range(FEATS):
+        dense_ref[f] = pick(stage[CAP * f : CAP * (f + 1), :], found_row, found_lane)
 
     finish_send(ask, True, 0)
-    finish_send(ask, False, 1)
+    passed.wait_send()
     finish_send(rowsend, True, 2)
     finish_send(gsend, True, 3)
     finish_send(gsend, False, 4)
     greeting.wait()
 
 
-def owner_kernel(params_ref, dense_ref, cams_ref, grads_ref, pv, gv, in_sem, out_sem):
+def owner_kernel(
+    params_ref, dense_ref, cams_ref, image_ref, grads_ref, rendered_ref, pv, gv, in_sem, out_sem
+):
+    rendered_ref[...] = image_ref[...]
     loads = [
         pltpu.make_async_copy(
             params_ref.at[:, pl.ds(128 * b, 128)], pv.at[pl.ds(PITCH * b, ROWS)], in_sem.at[b]
@@ -590,18 +623,24 @@
 
 def on_device(params, camera, eye_point, tile_of, fetch, lists, counts, target):
     vmem = pl.BlockSpec(memory_space=pltpu.VMEM)
-    smem = pl.BlockSpec(memory_space=pltpu.SMEM)
-    hbm = pl.BlockSpec(memory_space=pl.ANY)
-    rendered, dense, cams = pl.pallas_call(
+    hbm = pl.BlockSpec(memory_space=pltpu.HBM)
+    image, dense, cams = pl.pallas_call(
         render_kernel,
         out_shape=(
-            jax.ShapeDtypeStruct((TILES, 3, PX), F32),
+            jax.ShapeDtypeStruct((3, TILES, PX), F32),
             jax.ShapeDtypeStruct((FEATS + 1, COLS, 128), F32),
             jax.ShapeDtypeStruct((16, 128), F32),
         ),
-        in_specs=[hbm, smem, smem, vmem, vmem, smem, smem, vmem, vmem, vmem],
+        in_specs=[hbm] * 8,
         out_specs=(vmem, vmem, vmem),
         scratch_shapes=[
+            pltpu.SMEM((3, 1, 4), F32),
+            pltpu.SMEM((1, 3), F32),
+            pltpu.SMEM((1, TILES), jnp.int32),
+            pltpu.SMEM((1, TILES), jnp.int32),
+            pltpu.VMEM((CAP, N), jnp.int32),
+            pltpu.VMEM((TILES, K), jnp.int32),
+            pltpu.VMEM((3, TILES, PX), F32),
             pltpu.VMEM((COLS * PITCH, 128), F32),
             pltpu.VMEM((FEATS, COLS, 128), F32),
             pltpu.VMEM((N, 128), jnp.int32),
@@ -621,42 +660,46 @@
             pltpu.VMEM((1, 128), jnp.int32),
             pltpu.VMEM((1, 256), F32),
             pltpu.VMEM((1, 256), F32),
+            pltpu.VMEM((TILES, CAP, K), BF16),
+            pltpu.VMEM((TILES, N, K), BF16),
+            pltpu.SemaphoreType.DMA((7,)),
             pltpu.SemaphoreType.DMA((2,)),
             pltpu.SemaphoreType.DMA((COLS,)),
             pltpu.SemaphoreType.DMA((5,)),
             pltpu.SemaphoreType.DMA((5,)),
         ],
         compiler_params=pltpu.CompilerParams(
-            collective_id=0, has_side_effects=True, vmem_limit_bytes=40 << 20
+            collective_id=0, has_side_effects=True, vmem_limit_bytes=56 << 20
         ),
         name="render",
     )(
         params,
-        camera[0],
-        eye_point,
-        camera[0],
+        camera.transpose(1, 0, 2),
         eye_point,
         tile_of,
         counts,
-        fetch[0, 0],
+        fetch[0, 0].T,
         lists[0],
-        target[0],
+        target[0].transpose(1, 0, 2),
     )
-    grads = pl.pallas_call(
+    grads, rendered = pl.pallas_call(
         owner_kernel,
-        out_shape=jax.ShapeDtypeStruct(params.shape, F32),
-        in_specs=[hbm, vmem, vmem],
-        out_specs=hbm,
+        out_shape=(
+            jax.ShapeDtypeStruct(params.shape, F32),
+            jax.ShapeDtypeStruct(image.shape, F32),
+        ),
+        in_specs=[hbm, vmem, vmem, vmem],
+        out_specs=(hbm, vmem),
         scratch_shapes=[
             pltpu.VMEM((COLS * PITCH, 128), F32),
             pltpu.VMEM((COLS * PITCH, 128), F32),
             pltpu.SemaphoreType.DMA((COLS,)),
             pltpu.SemaphoreType.DMA((COLS,)),
         ],
-        compiler_params=pltpu.CompilerParams(vmem_limit_bytes=32 << 20),
+        compiler_params=pltpu.CompilerParams(vmem_limit_bytes=56 << 20),
         name="owner",
-    )(params, dense, cams)
-    return (rendered[None], grads)
+    )(params, dense, cams, image)
+    return (rendered.transpose(1, 0, 2)[None], grads)
 
 
 def solution(mesh):

time: 49 us -> 40.6 us (0.83)
  Pallas kernels: 44.3 us -> 39.6 us
  local copies, waits for them, and re-layouts: 3.81 us -> 0 us
    pallas_call x2, Pallas kernels: 44.3 us -> 39.6 us  [the longest x1 35.2 us: on_device(): pl.pallas_call(render_kernel, out_shape=(jax.ShapeDtypeStruct((3, TILES,...]
    unnamed x18 -> x0, local copies, waits for them, and re-layouts: 3.81 us -> none
where the time goes in v2:
time: 40.6 us; the launch traced here: 40.3 us
  Pallas kernels  39.6 us (98%)
  between operations  0.64 us (2%)
    pallas_call x1, Pallas kernels, on_device(): pl.pallas_call(render_kernel, out_shape=(jax.ShapeDtypeStruct((3, TILES,...  35.2 us
    pallas_call x1, Pallas kernels, on_device(): pl.pallas_call(owner_kernel, out_shape=(jax.ShapeDtypeStruct(params.shape...  4.46 us

profile of v2, /device:TPU:1, one launch (start us, length us, event | category | flops | bytes accessed | tf_op | source)
XLA Modules:
  0.0 40.3 jit_solution(13437380641962382267)
XLA Ops:
  0.6 35.2 %render.1 = (f32[3,8,256]{2,1,0:T(8,128)}, f32[10,16,128]{2,1,0:T(8,128)}, f32[16,128]{1,0:T(8,128)}) custom-call(f32[59,2048]{1,0:T(8,128)} %params_ref.1, f32[3,1,4]{2,1,0:T(1,128)} %bitcast.14, f32[1,3]{1,0:T(1,128)} %eye_hbm.1, s32[1,8]{1,0:T(1,128)} %tile_hbm.1, s32[1,8]{1,0:T(1,128)} %count_hbm.1, s32[16,64]{1,0:T(8,128)} %bitcast.12, ...), custom_call_target="tpu_custom_call" | custom-call | tf_op jit(solution)/shard_map/render/pallas_call | solution.py:627
  35.8 4.5 %owner.1 = (f32[59,2048]{1,0:T(8,128)}, f32[3,8,256]{2,1,0:T(8,128)}) custom-call(f32[59,2048]{1,0:T(8,128)} %params_ref.1, f32[10,16,128]{2,1,0:T(8,128)} %get-tuple-element.7.dense_ref, f32[16,128]{1,0:T(8,128)} %get-tuple-element.8.cams_ref, f32[3,8,256]{2,1,0:T(8,128)} %get-tuple-element.9.image_ref), custom_call_target="tpu_custom_call" | custom-call | tf_op jit(solution)/shard_map/owner/pallas_call | solution.py:685

commit v3 on v2

--- a/solution.py
+++ b/solution.py
@@ -179,7 +179,7 @@
     lists_hbm,
     target_hbm,
     rendered_ref,
-    dense_ref,
+    grads_ref,
     cams_ref,
     cam_ref,
     eye_ref,
@@ -380,7 +380,7 @@
     found = lax.fori_loop(0, CAP, locate, jnp.zeros((2 * COLS, 128), F32))
     found_row = found[0:COLS].astype(jnp.int32)
     found_lane = found[COLS : 2 * COLS].astype(jnp.int32)
-    dense_ref[FEATS] = jnp.where(found_lane < N, 1.0, 0.0)
+    own = found_lane < N
 
     pixel = iota((TILES, PX), 1)
     u = (pixel % 16).astype(F32) - 7.5
@@ -564,34 +564,8 @@
     exchange(gsend, gin, True, 3)
     keep(gsend, gin, spare_grads, 3)
     exchange(gsend, gin, False, 4)
-    finish_recv(gin, True, 3)
-    finish_recv(gin, False, 4)
-    stage[...] = gin[...].T
-
-    for f in range(FEATS):
-        dense_ref[f] = pick(stage[CAP * f : CAP * (f + 1), :], found_row, found_lane)
-
-    finish_send(ask, True, 0)
-    passed.wait_send()
-    finish_send(rowsend, True, 2)
-    finish_send(gsend, True, 3)
-    finish_send(gsend, False, 4)
-    greeting.wait()
-
-
-def owner_kernel(
-    params_ref, dense_ref, cams_ref, image_ref, grads_ref, rendered_ref, pv, gv, in_sem, out_sem
-):
-    rendered_ref[...] = image_ref[...]
-    loads = [
-        pltpu.make_async_copy(
-            params_ref.at[:, pl.ds(128 * b, 128)], pv.at[pl.ds(PITCH * b, ROWS)], in_sem.at[b]
-        )
-        for b in range(COLS)
-    ]
-    for load in loads:
-        load.start()
-    own = dense_ref[FEATS] > 0.5
+
+    greeting.wait_recv()
 
     def chosen(row, col):
         return jnp.where(
@@ -602,38 +576,54 @@
 
     camera = [[chosen(r, c) for c in range(4)] for r in range(2)]
     eye = [chosen(3, c) for c in range(3)]
-    for load in loads:
-        load.wait()
     values = [pv[pl.ds(p, COLS, stride=PITCH), :] for p in range(ROWS)]
     _, pull = jax.vjp(lambda rows: project(rows, camera, eye), values)
-    (grads,) = pull([dense_ref[f] for f in range(FEATS)])
+
+    finish_recv(gin, True, 3)
+    finish_recv(gin, False, 4)
+    stage[...] = gin[...].T
+
+    found = [
+        pick(stage[CAP * f : CAP * (f + 1), :], found_row, found_lane) for f in range(FEATS)
+    ]
+    (grads,) = pull(found)
     for p in range(ROWS):
-        gv[pl.ds(p, COLS, stride=PITCH), :] = grads[p]
-    stores = [
+        grads_ref[pl.ds(p, COLS, stride=PITCH), :] = grads[p]
+    finish_send(ask, True, 0)
+    passed.wait_send()
+    finish_send(rowsend, True, 2)
+    finish_send(gsend, True, 3)
+    finish_send(gsend, False, 4)
+    greeting.wait_send()
+
+
+def hand_on(image_ref, blocks_ref, image_hbm, grads_hbm, sems):
+    copies = [
         pltpu.make_async_copy(
-            gv.at[pl.ds(PITCH * b, ROWS)], grads_ref.at[:, pl.ds(128 * b, 128)], out_sem.at[b]
+            blocks_ref.at[pl.ds(PITCH * b, ROWS)], grads_hbm.at[:, pl.ds(128 * b, 128)], sems.at[b]
         )
         for b in range(COLS)
     ]
-    for store in stores:
-        store.start()
-    for store in stores:
-        store.wait()
+    copies.append(pltpu.make_async_copy(image_ref, image_hbm, sems.at[COLS]))
+    for copy in copies:
+        copy.start()
+    for copy in copies:
+        copy.wait()
 
 
 def on_device(params, camera, eye_point, tile_of, fetch, lists, counts, target):
     vmem = pl.BlockSpec(memory_space=pltpu.VMEM)
     hbm = pl.BlockSpec(memory_space=pltpu.HBM)
-    image, dense, cams = pl.pallas_call(
+    image, blocks = pl.pallas_call(
         render_kernel,
         out_shape=(
-            jax.ShapeDtypeStruct((3, TILES, PX), F32),
-            jax.ShapeDtypeStruct((FEATS + 1, COLS, 128), F32),
-            jax.ShapeDtypeStruct((16, 128), F32),
+            pltpu.VMEM((3, TILES, PX), F32),
+            pltpu.VMEM((COLS * PITCH, 128), F32),
         ),
         in_specs=[hbm] * 8,
-        out_specs=(vmem, vmem, vmem),
+        out_specs=(vmem, vmem),
         scratch_shapes=[
+            pltpu.VMEM((16, 128), F32),
             pltpu.SMEM((3, 1, 4), F32),
             pltpu.SMEM((1, 3), F32),
             pltpu.SMEM((1, TILES), jnp.int32),
@@ -669,36 +659,36 @@
             pltpu.SemaphoreType.DMA((5,)),
         ],
         compiler_params=pltpu.CompilerParams(
-            collective_id=0, has_side_effects=True, vmem_limit_bytes=56 << 20
+            collective_id=0, has_side_effects=True, vmem_limit_bytes=40 << 20
         ),
         name="render",
     )(
-        params,
-        camera.transpose(1, 0, 2),
-        eye_point,
-        tile_of,
-        counts,
-        fetch[0, 0].T,
-        lists[0],
-        target[0].transpose(1, 0, 2),
+        *[
+            pltpu.with_memory_space_constraint(arg, pltpu.HBM)
+            for arg in (
+                params,
+                camera.transpose(1, 0, 2),
+                eye_point,
+                tile_of,
+                counts,
+                fetch[0, 0].T,
+                lists[0],
+                target[0].transpose(1, 0, 2),
+            )
+        ]
     )
-    grads, rendered = pl.pallas_call(
-        owner_kernel,
+    rendered, grads = pl.pallas_call(
+        hand_on,
         out_shape=(
+            jax.ShapeDtypeStruct(image.shape, F32),
             jax.ShapeDtypeStruct(params.shape, F32),
-            jax.ShapeDtypeStruct(image.shape, F32),
         ),
-        in_specs=[hbm, vmem, vmem, vmem],
-        out_specs=(hbm, vmem),
-        scratch_shapes=[
-            pltpu.VMEM((COLS * PITCH, 128), F32),
-            pltpu.VMEM((COLS * PITCH, 128), F32),
-            pltpu.SemaphoreType.DMA((COLS,)),
-            pltpu.SemaphoreType.DMA((COLS,)),
-        ],
-        compiler_params=pltpu.CompilerParams(vmem_limit_bytes=56 << 20),
-        name="owner",
-    )(params, dense, cams, image)
+        in_specs=[pl.BlockSpec(memory_space=pl.ANY)] * 2,
+        out_specs=(hbm, hbm),
+        scratch_shapes=[pltpu.SemaphoreType.DMA((COLS + 1,))],
+        compiler_params=pltpu.CompilerParams(vmem_limit_bytes=4 << 20),
+        name="hand_on",
+    )(*[pltpu.with_memory_space_constraint(x, pltpu.VMEM) for x in (image, blocks)])
     return (rendered.transpose(1, 0, 2)[None], grads)
 
 

time: 40.6 us -> 36.5 us (0.90)
  Pallas kernels: 39.6 us -> 35.7 us
    pallas_call x2, Pallas kernels: 39.6 us -> 35.7 us  [the longest x1 34.8 us: on_device(): pl.pallas_call(render_kernel, out_shape=(pltpu.VMEM((3, TILES, PX), F32),...]
where the time goes in v3:
time: 36.5 us; the launch traced here: 36.4 us
  Pallas kernels  35.7 us (98%)
  between operations  0.64 us (2%)
    pallas_call x1, Pallas kernels, on_device(): pl.pallas_call(render_kernel, out_shape=(pltpu.VMEM((3, TILES, PX), F32),...  34.8 us
    pallas_call x1, Pallas kernels, on_device(): pl.pallas_call(hand_on, out_shape=(jax.ShapeDtypeStruct(image.shape, F32)...  0.96 us

profile of v3, /device:TPU:1, one launch (start us, length us, event | category | flops | bytes accessed | tf_op | source)
XLA Modules:
  0.0 36.4 jit_solution(12650044556169386251)
XLA Ops:
  0.6 34.8 %render.1 = (f32[3,8,256]{2,1,0:T(8,128)S(1)}, f32[1024,128]{1,0:T(8,128)S(1)}) custom-call(f32[59,2048]{1,0:T(8,128)} %params_hbm.1, f32[3,1,4]{2,1,0:T(1,128)} %bitcast.14, f32[1,3]{1,0:T(1,128)} %eye_hbm.1, s32[1,8]{1,0:T(1,128)} %tile_hbm.1, s32[1,8]{1,0:T(1,128)} %count_hbm.1, s32[16,64]{1,0:T(8,128)} %bitcast.12, s32[8,256]{1,0:T(8,128)} %bitcast.13, ...), custom_call_target="tpu_custom_call" | custom-call | tf_op jit(solution)/shard_map/render/pallas_call | solution.py:617
  35.4 1.0 %hand_on.1 = (f32[3,8,256]{2,1,0:T(8,128)}, f32[59,2048]{1,0:T(8,128)}) custom-call(f32[3,8,256]{2,1,0:T(8,128)S(1)} %get-tuple-element.6.image_ref, f32[1024,128]{1,0:T(8,128)S(1)} %get-tuple-element.7.blocks_ref), custom_call_target="tpu_custom_call" | custom-call | tf_op jit(solution)/shard_map/hand_on/pallas_call | solution.py:680

commit v4 on v3

--- a/solution.py
+++ b/solution.py
@@ -43,8 +43,16 @@
 GROUP = 32
 MOMS = 16
 CHUNK = 32
-UNROLL_F = 8
-UNROLL_B = 8
+
+
+def hops(offset):
+    return sum(min(step, 4 - step) for step in offset)
+
+
+OFFSETS = sorted(
+    [(dz, dy, dx) for dz in range(4) for dy in range(4) for dx in range(4)],
+    key=lambda offset: (-hops(offset), offset),
+)
 
 
 def harmonics(dir_x, dir_y, dir_z):
@@ -209,6 +217,10 @@
     spare_grads,
     pos_ones,
     own_ones,
+    totals,
+    tones,
+    paints,
+    pieces,
     in_sems,
     cam_sem,
     par_sem,
@@ -218,6 +230,11 @@
     me = lax.axis_index("space")
     view = lax.axis_index("view")
     other = 1 - view
+    along = [(me // 16, 16), (me // 4 % 4, 4), (me % 4, 1)]
+    shifted = [[(at + step) % 4 * pitch for step in range(4)] for at, pitch in along]
+
+    def device(offset):
+        return sum(shifted[axis][step] for axis, step in enumerate(offset))
 
     def blank():
         stage[...] = jnp.zeros(stage.shape, F32)
@@ -252,13 +269,10 @@
     barrier = pltpu.get_barrier_semaphore()
     pl.semaphore_signal(barrier, inc=1, device_id=(me, other), device_id_type=MESH)
 
-    def greet(d, c):
+    for offset in OFFSETS[: N - 1]:
         pl.semaphore_signal(
-            barrier, inc=1, device_id=(lax.rem(me + d, N), view), device_id_type=MESH
+            barrier, inc=1, device_id=(device(offset), view), device_id_type=MESH
         )
-        return c
-
-    lax.fori_loop(1, N, greet, 0, unroll=7)
     loads = [
         pltpu.make_async_copy(
             params_hbm.at[:, pl.ds(128 * b, 128)], pv.at[pl.ds(PITCH * b, ROWS)], par_sem.at[b]
@@ -284,17 +298,14 @@
         )
 
     def exchange(src, dst, own, sems):
-        def one(d, c):
-            t = lax.rem(me + d, N)
+        for offset in OFFSETS[: N - 1] if own else OFFSETS:
+            t = device(offset)
             push(
                 src.at[pl.ds(t, 1)],
                 dst.at[pl.ds(me if own else N + me, 1)],
                 (t, view if own else other),
                 sems,
             ).start()
-            return c
-
-        lax.fori_loop(1 if own else 0, N, one, 0, unroll=7 if own else 8)
 
     def finish_send(src, own, sems):
         push(src, src, (me, view), sems).wait_send()
@@ -455,32 +466,45 @@
     chooser = jnp.where(adds & (wants < 3), 1.0, 0.0).astype(BF16)
     group_mask = iota((TILES, TILES * GROUP), 1) // GROUP == iota((TILES, TILES * GROUP), 0)
 
-    def forward(step, carry):
-        through, images = carry[0], list(carry[1:])
-        first = pl.multiple_of(step * CHUNK, CHUNK)
-        rows = pl.ds(pl.multiple_of(step * CHUNK * TILES, CHUNK * TILES), CHUNK * TILES)
-        spread = jnp.where(
-            group_mask[None], lanes[pl.ds(first, CHUNK), :][:, None, :], 0.0
-        ).reshape(CHUNK * TILES, TILES * GROUP)
-        low = spread.astype(BF16)
-        lhs[rows, :] = low
-        power = jnp.dot(low, rhs[...], preferred_element_type=F32)
-        paint = jnp.dot(low, chooser, preferred_element_type=F32)
-        alpha_all = jnp.exp2(power)
-        alphas[rows, :] = alpha_all
-        for i in range(CHUNK):
-            alpha = alpha_all[i * TILES : (i + 1) * TILES]
-            weight = through * alpha
-            through = through * (1.0 - alpha)
-            at = pl.ds(pl.multiple_of((first + i) * TILES, TILES), TILES)
-            weights[at, :] = weight
-            for c in range(3):
-                shine = paint[i * TILES : (i + 1) * TILES, c : c + 1]
-                images[c] = images[c] + weight * shine
-        return (through, *images)
-
-    zero = jnp.zeros((TILES, PX), F32)
-    _, *images = lax.fori_loop(0, K // CHUNK, forward, (jnp.ones((TILES, PX), F32), zero, zero, zero), unroll=UNROLL_F)
+    def chunk_rows(chunk):
+        return slice(chunk * CHUNK * TILES, (chunk + 1) * CHUNK * TILES)
+
+    def operands(chunk):
+        line = lanes[chunk * CHUNK : (chunk + 1) * CHUNK, :]
+        spread = jnp.where(group_mask[None], line[:, None, :], 0.0)
+        lhs[chunk_rows(chunk), :] = spread.reshape(CHUNK * TILES, TILES * GROUP).astype(BF16)
+
+    def exponents(chunk):
+        rows = chunk_rows(chunk)
+        power = jnp.dot(lhs[rows, :], rhs[...], preferred_element_type=F32)
+        alphas[rows, :] = jnp.exp2(power)
+        paints[rows, :] = jnp.dot(lhs[rows, :], chooser, preferred_element_type=F32)
+
+    through = jnp.ones((TILES, PX), F32)
+    images = [jnp.zeros((TILES, PX), F32)] * 3
+    chunks = K // CHUNK
+    for stage_no in range(chunks + 2):
+        if stage_no < chunks:
+            operands(stage_no)
+        if 1 <= stage_no <= chunks:
+            exponents(stage_no - 1)
+        if stage_no >= 2:
+            first = (stage_no - 2) * CHUNK * TILES
+            for i in range(0, CHUNK, 2):
+                pair = []
+                for j in (i, i + 1):
+                    at = slice(first + j * TILES, first + (j + 1) * TILES)
+                    alpha = alphas[at, :]
+                    weight = through * alpha
+                    through = through * (1.0 - alpha)
+                    weights[at, :] = weight
+                    pair.append(weight)
+                    for c in range(3):
+                        images[c] = images[c] + weight * paints[at, c : c + 1]
+                at = slice(first + i * TILES, first + (i + 2) * TILES)
+                high, low = split_low(jnp.concatenate(pair, axis=0), 2)
+                pieces[at, 2 * PX : 3 * PX] = high
+                pieces[at, 3 * PX : 4 * PX] = low
 
     blank()
     shades = []
@@ -500,34 +524,41 @@
             lay(128 + 6 + 3 * c + part, MOMS, shades[c][part])
     moment_rows = staged(slice(0, 128)).astype(BF16)
     shade_rows = staged(slice(128, 256)).astype(BF16)
-    moment_mask = iota((TILES, 128), 1) // MOMS == iota((TILES, 128), 0)
-
-    def backward(back, behind):
-        step = K // CHUNK - 1 - back
-        first = pl.multiple_of(step * CHUNK, CHUNK)
-        rows = pl.ds(pl.multiple_of(step * CHUNK * TILES, CHUNK * TILES), CHUNK * TILES)
-        tone = jnp.dot(lhs[rows, :], rhs[...], preferred_element_type=F32)
-        alpha = alphas[rows, :]
-        weight = weights[rows, :]
-        slopes = [None] * CHUNK
-        for i in reversed(range(CHUNK)):
-            at = slice(i * TILES, (i + 1) * TILES)
-            gap = tone[at] - behind
-            slopes[i] = weight[at] * gap
-            behind = behind * (1.0 - alpha[at]) + alpha[at] * tone[at]
-        slope = jnp.concatenate(slopes, axis=0)
-        total = jnp.zeros((CHUNK * TILES, 128), F32)
-        for piece in split_low(slope, 2):
-            total = total + dot_nt(piece, moment_rows)
-        for piece in split_low(weight, 2):
-            total = total + dot_nt(piece, shade_rows)
-        total = jnp.where(moment_mask[None], total.reshape(CHUNK, TILES, 128), 0.0)
-        lanes[pl.ds(first, CHUNK), 0:128] = jnp.sum(total, axis=1)
-        return behind
-
-    lax.fori_loop(0, K // CHUNK, backward, zero, unroll=UNROLL_B)
-
-    turned_sums = lanes[:, 0:128].T
+    both_rows = jnp.concatenate([moment_rows, moment_rows, shade_rows, shade_rows], axis=1)
+
+    def tone_of(chunk):
+        rows = chunk_rows(chunk)
+        tones[rows, :] = jnp.dot(lhs[rows, :], rhs[...], preferred_element_type=F32)
+
+    def reductions(chunk):
+        rows = chunk_rows(chunk)
+        totals[rows, :] = dot_nt(pieces[rows, :], both_rows)
+
+    behind = jnp.zeros((TILES, PX), F32)
+    for stage_no in range(chunks + 2):
+        if stage_no < chunks:
+            tone_of(chunks - 1 - stage_no)
+        if stage_no >= 2:
+            reductions(chunks + 1 - stage_no)
+        if 1 <= stage_no <= chunks:
+            first = (chunks - stage_no) * CHUNK * TILES
+            for i in reversed(range(0, CHUNK, 2)):
+                pair = [None, None]
+                for j in (1, 0):
+                    at = slice(first + (i + j) * TILES, first + (i + j + 1) * TILES)
+                    tone, alpha = tones[at, :], alphas[at, :]
+                    pair[j] = weights[at, :] * (tone - behind)
+                    behind = behind * (1.0 - alpha) + alpha * tone
+                at = slice(first + i * TILES, first + (i + 2) * TILES)
+                high, low = split_low(jnp.concatenate(pair, axis=0), 2)
+                pieces[at, 0:PX] = high
+                pieces[at, PX : 2 * PX] = low
+
+    group = iota((K, 128), 1) // MOMS
+    sums = totals[pl.ds(0, K, stride=TILES), :]
+    for t in range(1, TILES):
+        sums = jnp.where(group == t, totals[pl.ds(t, K, stride=TILES), :], sums)
+    turned_sums = sums.T
     stage[0:128, :] = turned_sums[:, 0:128]
     stage_hi[0:128, :] = turned_sums[:, 128:256]
     sums = [take(c, MOMS) for c in range(15)]
@@ -652,6 +683,10 @@
             pltpu.VMEM((1, 256), F32),
             pltpu.VMEM((TILES, CAP, K), BF16),
             pltpu.VMEM((TILES, N, K), BF16),
+            pltpu.VMEM((K * TILES, 128), F32),
+            pltpu.VMEM((K * TILES, PX), F32),
+            pltpu.VMEM((K * TILES, 128), F32),
+            pltpu.VMEM((K * TILES, 4 * PX), BF16),
             pltpu.SemaphoreType.DMA((7,)),
             pltpu.SemaphoreType.DMA((2,)),
             pltpu.SemaphoreType.DMA((COLS,)),

time: 36.5 us -> 34.9 us (0.956)
  Pallas kernels: 35.7 us -> 34.1 us
    pallas_call x1, Pallas kernels: 34.8 us -> 33.1 us  [on_device(): pl.pallas_call(render_kernel, out_shape=(pltpu.VMEM((3, TILES, PX), F32),...]
where the time goes in v4:
time: 34.9 us; the launch traced here: 34.8 us
  Pallas kernels  34.1 us (98%)
  between operations  0.64 us (2%)
    pallas_call x1, Pallas kernels, on_device(): pl.pallas_call(render_kernel, out_shape=(pltpu.VMEM((3, TILES, PX), F32),...  33.1 us
    pallas_call x1, Pallas kernels, on_device(): pl.pallas_call(hand_on, out_shape=(jax.ShapeDtypeStruct(image.shape, F32)...  0.96 us

profile of v4, /device:TPU:1, one launch (start us, length us, event | category | flops | bytes accessed | tf_op | source)
XLA Modules:
  0.0 34.8 jit_solution(13692491359717440163)
XLA Ops:
  0.6 33.1 %render.1 = (f32[3,8,256]{2,1,0:T(8,128)S(1)}, f32[1024,128]{1,0:T(8,128)S(1)}) custom-call(f32[59,2048]{1,0:T(8,128)} %params_hbm.1, f32[3,1,4]{2,1,0:T(1,128)} %bitcast.14, f32[1,3]{1,0:T(1,128)} %eye_hbm.1, s32[1,8]{1,0:T(1,128)} %tile_hbm.1, s32[1,8]{1,0:T(1,128)} %count_hbm.1, s32[16,64]{1,0:T(8,128)} %bitcast.12, s32[8,256]{1,0:T(8,128)} %bitcast.13, ...), custom_call_target="tpu_custom_call" | custom-call | tf_op jit(solution)/shard_map/render/pallas_call | solution.py:648
  33.8 1.0 %hand_on.1 = (f32[3,8,256]{2,1,0:T(8,128)}, f32[59,2048]{1,0:T(8,128)}) custom-call(f32[3,8,256]{2,1,0:T(8,128)S(1)} %get-tuple-element.6.image_ref, f32[1024,128]{1,0:T(8,128)S(1)} %get-tuple-element.7.blocks_ref), custom_call_target="tpu_custom_call" | custom-call | tf_op jit(solution)/shard_map/hand_on/pallas_call | solution.py:715

commit v5 on v4

--- a/solution.py
+++ b/solution.py
@@ -218,6 +218,13 @@
     pos_ones,
     own_ones,
     totals,
+    coef_lo,
+    coef_hi,
+    tone_lo,
+    tone_hi,
+    shade_lo,
+    shade_hi,
+    both_rows,
     tones,
     paints,
     pieces,
@@ -236,20 +243,23 @@
     def device(offset):
         return sum(shifted[axis][step] for axis, step in enumerate(offset))
 
+    places = [(stage, stage_hi), (coef_lo, coef_hi), (tone_lo, tone_hi), (shade_lo, shade_hi)]
+
     def blank():
         stage[...] = jnp.zeros(stage.shape, F32)
         stage_hi[...] = jnp.zeros(stage.shape, F32)
 
-    def lay(first, stride, value):
-        stage[pl.ds(first, TILES, stride=stride), :] = value[:, 0:128]
-        stage_hi[pl.ds(first, TILES, stride=stride), :] = value[:, 128:256]
+    def lay(first, stride, value, where=0):
+        low, high = places[where]
+        low[pl.ds(first, TILES, stride=stride), :] = value[:, 0:128]
+        high[pl.ds(first, TILES, stride=stride), :] = value[:, 128:256]
 
     def take(first, stride):
         rows = pl.ds(first, TILES, stride=stride)
         return jnp.concatenate([stage[rows, :], stage_hi[rows, :]], axis=1)
 
-    def staged(rows=slice(None)):
-        return jnp.concatenate([stage[rows, :], stage_hi[rows, :]], axis=1)
+    def staged(rows=slice(None), where=0):
+        return jnp.concatenate([part[rows, :] for part in places[where]], axis=1)
 
     small = [
         pltpu.make_async_copy(src, dst, in_sems.at[i])
@@ -402,6 +412,15 @@
         for part in range(3):
             lay(3 * c + part, GROUP, basis[c])
     rhs[...] = staged().astype(BF16)
+    blank()
+    for c in range(6):
+        lay(c, MOMS, basis[c])
+    both_rows[:, 0:PX] = staged(slice(0, 128)).astype(BF16)
+    both_rows[:, PX : 2 * PX] = staged(slice(0, 128)).astype(BF16)
+    for pair in places[1:]:
+        for part in pair:
+            part[...] = jnp.zeros(part.shape, F32)
+    gsend[...] = jnp.zeros(gsend.shape, F32)
 
     for t in range(TILES):
         listed = lists_ref[t : t + 1, :]
@@ -447,23 +466,22 @@
     lin_y = con_c * spot_y + con_b * spot_x
     level = entries[5] - 0.5 * (spot_x * lin_x + spot_y * lin_y)
     coeffs = [level, lin_x, lin_y, -0.5 * con_a, -con_b, -0.5 * con_c]
-    blank()
     for c in range(6):
         coeff = jnp.where(alive, coeffs[c] * LOG2E, -1e30 if c == 0 else 0.0)
         for part, piece in enumerate(split(coeff, 3)):
-            lay(3 * c + part, GROUP, piece)
+            lay(3 * c + part, GROUP, piece, 1)
     colours = [jnp.where(alive, entries[6 + c], 0.0) for c in range(3)]
     for c in range(3):
         high, low, rest = split(colours[c], 3)
         for part, piece in enumerate((high, high, low)):
-            lay(18 + 3 * c + part, GROUP, piece)
-        lay(27 + c, GROUP, rest)
-    lanes[...] = staged().T
-
-    column = iota((TILES * GROUP, 128), 0) % GROUP
-    wants = iota((TILES * GROUP, 128), 1)
+            lay(18 + 3 * c + part, GROUP, piece, 1)
+        lay(27 + c, GROUP, rest, 1)
+    lanes[...] = staged(where=1).T
+
+    column = iota((TILES * GROUP, 3 * 128), 0) % GROUP
+    wants = iota((TILES * GROUP, 3 * 128), 1) // 128
     adds = (column == 18 + 3 * wants) | (column == 20 + 3 * wants) | (column == 27 + wants)
-    chooser = jnp.where(adds & (wants < 3), 1.0, 0.0).astype(BF16)
+    chooser = jnp.where(adds, 1.0, 0.0).astype(BF16)
     group_mask = iota((TILES, TILES * GROUP), 1) // GROUP == iota((TILES, TILES * GROUP), 0)
 
     def chunk_rows(chunk):
@@ -500,31 +518,24 @@
                     weights[at, :] = weight
                     pair.append(weight)
                     for c in range(3):
-                        images[c] = images[c] + weight * paints[at, c : c + 1]
+                        paint = paints[at, 128 * c : 128 * c + 128]
+                        images[c] = images[c] + weight * jnp.concatenate([paint, paint], axis=1)
                 at = slice(first + i * TILES, first + (i + 2) * TILES)
                 high, low = split_low(jnp.concatenate(pair, axis=0), 2)
                 pieces[at, 2 * PX : 3 * PX] = high
                 pieces[at, 3 * PX : 4 * PX] = low
 
-    blank()
-    shades = []
     for c in range(3):
         rendered_ref[c] = images[c]
         shade = (images[c] - target_ref[c]) * (1.0 / 256.0)
         high, low = split(shade, 2)
-        shades.append(split(shade, 3))
         for part, piece in enumerate((high, low, high)):
-            lay(18 + 3 * c + part, GROUP, piece)
-    rhs[...] = staged().astype(BF16)
-    blank()
-    for c in range(6):
-        lay(c, MOMS, basis[c])
-    for c in range(3):
-        for part in range(3):
-            lay(128 + 6 + 3 * c + part, MOMS, shades[c][part])
-    moment_rows = staged(slice(0, 128)).astype(BF16)
-    shade_rows = staged(slice(128, 256)).astype(BF16)
-    both_rows = jnp.concatenate([moment_rows, moment_rows, shade_rows, shade_rows], axis=1)
+            lay(18 + 3 * c + part, GROUP, piece, 2)
+        for part, piece in enumerate(split(shade, 3)):
+            lay(6 + 3 * c + part, MOMS, piece, 3)
+    rhs[...] = staged(where=2).astype(BF16)
+    both_rows[:, 2 * PX : 3 * PX] = staged(where=3).astype(BF16)
+    both_rows[:, 3 * PX : 4 * PX] = staged(where=3).astype(BF16)
 
     def tone_of(chunk):
         rows = chunk_rows(chunk)
@@ -532,7 +543,7 @@
 
     def reductions(chunk):
         rows = chunk_rows(chunk)
-        totals[rows, :] = dot_nt(pieces[rows, :], both_rows)
+        totals[rows, :] = dot_nt(pieces[rows, :], both_rows[...])
 
     behind = jnp.zeros((TILES, PX), F32)
     for stage_no in range(chunks + 2):
@@ -577,7 +588,6 @@
         s_1,
         *[sums[6 + 3 * c] + sums[7 + 3 * c] + sums[8 + 3 * c] for c in range(3)],
     ]
-    blank()
     for f in range(FEATS):
         for part, piece in enumerate(split(jnp.where(alive, slopes[f], 0.0), 2)):
             lay(FEATS * part + f, GROUP, piece)
@@ -589,12 +599,19 @@
         total = total + dot_nt(left.reshape(2 * FEATS * CAP, K), own_ones[t])
     size = FEATS * CAP
     summed = total[0:size] + total[size : 2 * size]
-    gsend[...] = jnp.zeros(gsend.shape, F32)
     gsend[:, 0:size] = summed.T
 
-    exchange(gsend, gin, True, 3)
+    for offset in OFFSETS:
+        t = device(offset)
+        for own_view in (True, False):
+            if any(offset) or not own_view:
+                push(
+                    gsend.at[pl.ds(t, 1)],
+                    gin.at[pl.ds(me if own_view else N + me, 1)],
+                    (t, view if own_view else other),
+                    3 if own_view else 4,
+                ).start()
     keep(gsend, gin, spare_grads, 3)
-    exchange(gsend, gin, False, 4)
 
     greeting.wait_recv()
 
@@ -684,8 +701,15 @@
             pltpu.VMEM((TILES, CAP, K), BF16),
             pltpu.VMEM((TILES, N, K), BF16),
             pltpu.VMEM((K * TILES, 128), F32),
+            pltpu.VMEM((TILES * GROUP, 128), F32),
+            pltpu.VMEM((TILES * GROUP, 128), F32),
+            pltpu.VMEM((TILES * GROUP, 128), F32),
+            pltpu.VMEM((TILES * GROUP, 128), F32),
+            pltpu.VMEM((TILES * MOMS, 128), F32),
+            pltpu.VMEM((TILES * MOMS, 128), F32),
+            pltpu.VMEM((TILES * MOMS, 4 * PX), BF16),
             pltpu.VMEM((K * TILES, PX), F32),
-            pltpu.VMEM((K * TILES, 128), F32),
+            pltpu.VMEM((K * TILES, 3 * 128), F32),
             pltpu.VMEM((K * TILES, 4 * PX), BF16),
             pltpu.SemaphoreType.DMA((7,)),
             pltpu.SemaphoreType.DMA((2,)),

time: 34.9 us -> 34.3 us (0.983)
  Pallas kernels: 34.1 us -> 33.5 us
    pallas_call x1, Pallas kernels: 33.1 us -> 32.5 us  [on_device(): pl.pallas_call(render_kernel, out_shape=(pltpu.VMEM((3, TILES, PX), F32),...]
where the time goes in v5:
time: 34.3 us; the launch traced here: 34.1 us
  Pallas kernels  33.5 us (98%)
  between operations  0.64 us (2%)
    pallas_call x1, Pallas kernels, on_device(): pl.pallas_call(render_kernel, out_shape=(pltpu.VMEM((3, TILES, PX), F32),...  32.5 us
    pallas_call x1, Pallas kernels, on_device(): pl.pallas_call(hand_on, out_shape=(jax.ShapeDtypeStruct(image.shape, F32)...  0.96 us

profile of v5, /device:TPU:1, one launch (start us, length us, event | category | flops | bytes accessed | tf_op | source)
XLA Modules:
  0.0 34.1 jit_solution(533531326470953224)
XLA Ops:
  0.6 32.5 %render.1 = (f32[3,8,256]{2,1,0:T(8,128)S(1)}, f32[1024,128]{1,0:T(8,128)S(1)}) custom-call(f32[59,2048]{1,0:T(8,128)} %params_hbm.1, f32[3,1,4]{2,1,0:T(1,128)} %bitcast.14, f32[1,3]{1,0:T(1,128)} %eye_hbm.1, s32[1,8]{1,0:T(1,128)} %tile_hbm.1, s32[1,8]{1,0:T(1,128)} %count_hbm.1, s32[16,64]{1,0:T(8,128)} %bitcast.12, s32[8,256]{1,0:T(8,128)} %bitcast.13, ...), custom_call_target="tpu_custom_call" | custom-call | tf_op jit(solution)/shard_map/render/pallas_call | solution.py:665
  33.2 1.0 %hand_on.1 = (f32[3,8,256]{2,1,0:T(8,128)}, f32[59,2048]{1,0:T(8,128)}) custom-call(f32[3,8,256]{2,1,0:T(8,128)S(1)} %get-tuple-element.6.image_ref, f32[1024,128]{1,0:T(8,128)S(1)} %get-tuple-element.7.blocks_ref), custom_call_target="tpu_custom_call" | custom-call | tf_op jit(solution)/shard_map/hand_on/pallas_call | solution.py:739

commit v6 on v5

--- a/solution.py
+++ b/solution.py
@@ -356,53 +356,6 @@
     )
     greeting.start()
 
-    finish_recv(req, True, 0)
-    wanted = req[0:N, :].T[0:CAP, :]
-    wanted = jnp.concatenate([wanted[0:8], wanted[8:16]], axis=1)
-    want_row, want_lane = wanted >> 7, wanted & 127
-    for f in range(FEATS):
-        found = pick(pj[f], want_row, want_lane)
-        stage[CAP * f : CAP * f + 8, :] = found
-        stage[CAP * f + 8 : CAP * (f + 1), :] = pltpu.roll(found, N, 1)
-    rowsend[...] = stage[...].T[0:N, :]
-    exchange(rowsend, rowsin, True, 2)
-    keep(rowsend, rowsin, spare_rows, 2)
-
-    passed = pltpu.make_async_remote_copy(
-        src_ref=req.at[pl.ds(0, N)],
-        dst_ref=req.at[pl.ds(N, N)],
-        send_sem=send_sems.at[1],
-        recv_sem=recv_sems.at[1],
-        device_id=(me, other),
-        device_id_type=MESH,
-    )
-    passed.start()
-
-    passed.wait_recv()
-    turned[...] = req[...].T[0:CAP, :]
-
-    def locate(j, found):
-        line = turned[pl.ds(j, 1), :]
-        line_hi, line_lo = line >> 7, line & 127
-        hit = iota((COLS, 128), 0) == jnp.broadcast_to(line_hi, (COLS, 128))
-        spot = iota((COLS, 128), 1).astype(F32)
-        digits = jnp.concatenate(
-            [
-                jnp.where(hit, j.astype(F32), 0.0),
-                jnp.where(hit, spot, 0.0),
-            ],
-            axis=0,
-        ).astype(BF16)
-        ones = jnp.where(
-            iota((128, 128), 0) == jnp.broadcast_to(line_lo, (128, 128)), 1.0, 0.0
-        ).astype(BF16)
-        return found + dot_nt(digits, ones)
-
-    found = lax.fori_loop(0, CAP, locate, jnp.zeros((2 * COLS, 128), F32))
-    found_row = found[0:COLS].astype(jnp.int32)
-    found_lane = found[COLS : 2 * COLS].astype(jnp.int32)
-    own = found_lane < N
-
     pixel = iota((TILES, PX), 1)
     u = (pixel % 16).astype(F32) - 7.5
     w = (pixel // 16).astype(F32) - 7.5
@@ -429,8 +382,31 @@
         pos_ones[t] = jnp.where(at_pos, 1.0, 0.0).astype(BF16)
         own_ones[t] = jnp.where(at_own, 1.0, 0.0).astype(BF16)
 
+    finish_recv(req, True, 0)
+    wanted = req[0:N, :].T[0:CAP, :]
+    wanted = jnp.concatenate([wanted[0:8], wanted[8:16]], axis=1)
+    want_row, want_lane = wanted >> 7, wanted & 127
+    for f in range(FEATS):
+        found = pick(pj[f], want_row, want_lane)
+        stage[CAP * f : CAP * f + 8, :] = found
+        stage[CAP * f + 8 : CAP * (f + 1), :] = pltpu.roll(found, N, 1)
+    rowsend[...] = stage[...].T[0:N, :]
+    exchange(rowsend, rowsin, True, 2)
+    keep(rowsend, rowsin, spare_rows, 2)
+
+    passed = pltpu.make_async_remote_copy(
+        src_ref=req.at[pl.ds(0, N)],
+        dst_ref=req.at[pl.ds(N, N)],
+        send_sem=send_sems.at[1],
+        recv_sem=recv_sems.at[1],
+        device_id=(me, other),
+        device_id_type=MESH,
+    )
+    passed.start()
+
     entry_row = lists_ref[...] & 7
     entry_lane = (lists_ref[...] >> 4) + ((lists_ref[...] & 8) << 3)
+    passed.wait_recv()
     finish_recv(rowsin, True, 2)
     stage[...] = rowsin[...].T
 
@@ -612,6 +588,30 @@
                     3 if own_view else 4,
                 ).start()
     keep(gsend, gin, spare_grads, 3)
+
+    turned[...] = req[...].T[0:CAP, :]
+
+    def locate(j, found):
+        line = turned[pl.ds(j, 1), :]
+        line_hi, line_lo = line >> 7, line & 127
+        hit = iota((COLS, 128), 0) == jnp.broadcast_to(line_hi, (COLS, 128))
+        spot = iota((COLS, 128), 1).astype(F32)
+        digits = jnp.concatenate(
+            [
+                jnp.where(hit, j.astype(F32), 0.0),
+                jnp.where(hit, spot, 0.0),
+            ],
+            axis=0,
+        ).astype(BF16)
+        ones = jnp.where(
+            iota((128, 128), 0) == jnp.broadcast_to(line_lo, (128, 128)), 1.0, 0.0
+        ).astype(BF16)
+        return found + dot_nt(digits, ones)
+
+    found = lax.fori_loop(0, CAP, locate, jnp.zeros((2 * COLS, 128), F32), unroll=4)
+    found_row = found[0:COLS].astype(jnp.int32)
+    found_lane = found[COLS : 2 * COLS].astype(jnp.int32)
+    own = found_lane < N
 
     greeting.wait_recv()
 

time: 34.3 us -> 34.3 us (level)
  no operation moved by 1% of the time
where the time goes in v6:
time: 34.3 us; the launch traced here: 34.1 us
  Pallas kernels  33.5 us (98%)
  between operations  0.64 us (2%)
    pallas_call x1, Pallas kernels, on_device(): pl.pallas_call(render_kernel, out_shape=(pltpu.VMEM((3, TILES, PX), F32),...  32.5 us
    pallas_call x1, Pallas kernels, on_device(): pl.pallas_call(hand_on, out_shape=(jax.ShapeDtypeStruct(image.shape, F32)...  0.96 us

profile of v6, /device:TPU:1, one launch (start us, length us, event | category | flops | bytes accessed | tf_op | source)
XLA Modules:
  0.0 34.1 jit_solution(9110168568845809240)
XLA Ops:
  0.6 32.5 %render.1 = (f32[3,8,256]{2,1,0:T(8,128)S(1)}, f32[1024,128]{1,0:T(8,128)S(1)}) custom-call(f32[59,2048]{1,0:T(8,128)} %params_hbm.1, f32[3,1,4]{2,1,0:T(1,128)} %bitcast.14, f32[1,3]{1,0:T(1,128)} %eye_hbm.1, s32[1,8]{1,0:T(1,128)} %tile_hbm.1, s32[1,8]{1,0:T(1,128)} %count_hbm.1, s32[16,64]{1,0:T(8,128)} %bitcast.12, s32[8,256]{1,0:T(8,128)} %bitcast.13, ...), custom_call_target="tpu_custom_call" | custom-call | tf_op jit(solution)/shard_map/render/pallas_call | solution.py:665
  33.2 1.0 %hand_on.1 = (f32[3,8,256]{2,1,0:T(8,128)}, f32[59,2048]{1,0:T(8,128)}) custom-call(f32[3,8,256]{2,1,0:T(8,128)S(1)} %get-tuple-element.6.image_ref, f32[1024,128]{1,0:T(8,128)S(1)} %get-tuple-element.7.blocks_ref), custom_call_target="tpu_custom_call" | custom-call | tf_op jit(solution)/shard_map/hand_on/pallas_call | solution.py:739
